TPU v7x, 512 devices: a whole 4x8x8 slice. The times are simulated.
512 devices in a mesh: pulse: 32 (over z_hi, y, core), tile: 16 (over x, z_lo).
Axes of the slice: x: 4, y: 8, z: 8 (z_hi: 2, z_lo: 4; z = z_hi * 4 + z_lo), core: 2. Of those that a mesh axis runs over, the one named last changes fastest.
Arguments:
- raw: bfloat16 [8192, 4, 2, 8192], P(('pulse', 'tile')), may hold values from -6 to 6
- chirp: bfloat16 [4, 2, 128], replicated, may hold values from -0.1875 to 0.1875
- steer: float32 [8192, 128], P('pulse'), may hold values from -3.140625 to 3.140625
- offsets: int32 [5, 2, 128], replicated, may hold values from 0 to 124, as said below
- interp: bfloat16 [5, 2, 2, 4, 2, 128], replicated, may hold values from -1.5 to 1.5
- owner: int32 [16], replicated, may hold values from 0 to 15, each once
Outputs:
- image: bfloat16 [2, 4096, 8192], P(None, 'pulse', 'tile')
Inputs may be any that keep to these rules, and one draw needn't show every extreme that they name: Each offsets[l, b, a] lies between (b * 128 + a) // 2 - 4 // 2 and (b * 128 + a) // 2 - 4 // 2 + 2, clipped to the range. `owner`: each tile holds a different range block.
All inputs are finite; a program needn't handle non-finite values.
Results may differ from a plain program's by a relative error of at most 0.0084.
Values may be sent and summed in bfloat16 or wider, within the bound.
No kernel may reach another device: no remote copies, remote signals or barrier semaphores. Data moves between devices by JAX's collectives and lax.ppermute only.
A program may use at most 64 MiB of HBM per device.

v0:
```python
import math

import jax
import jax.numpy as jnp
from jax import lax
from jax.sharding import PartitionSpec as P


def swapped(block, axis, apart):
    count = lax.axis_size(axis)
    route = []
    for low in range(count):
        high = low | 1 << apart
        if high != low and high < count:
            route += [(low, high), (high, low)]
    return lax.ppermute(block, axis, route)


def filter_table(chirp):
    taps = chirp.shape[2]
    channels = chirp.shape[0]
    padded = jnp.pad(chirp, ((0, 0), (0, 0), (0, taps + 1)))
    tiled = jnp.tile(padded, (1, 1, taps))[:, :, : taps * 2 * taps]
    skewed = tiled.reshape(channels, 2, taps, 2 * taps)
    picked = jnp.swapaxes(skewed, 2, 3)
    real_tap = picked[:, 0]
    imag_tap = picked[:, 1]
    from_real = jnp.stack([real_tap, imag_tap], axis=2)
    from_imag = jnp.stack([-imag_tap, real_tap], axis=2)
    return jnp.stack([from_real, from_imag], axis=1)


def complex_block(real_part, imag_part):
    upper = jnp.concatenate([real_part, -imag_part], axis=1)
    lower = jnp.concatenate([imag_part, real_part], axis=1)
    return jnp.concatenate([upper, lower], axis=0)


def steer_block(cos_cols, sin_cols):
    real_rows = jnp.stack([cos_cols, -sin_cols], axis=2)
    imag_rows = jnp.stack([sin_cols, cos_cols], axis=2)
    stacked = jnp.stack([real_rows, imag_rows], axis=0)
    return stacked.reshape(2 * cos_cols.shape[0], 2 * cos_cols.shape[1])


def band_matrix(tap_weights, onehot):
    hp = lax.Precision.HIGHEST
    values = tap_weights.astype(jnp.float32)
    real_part = jnp.einsum("ka,kab->ab", values[:, 0], onehot, precision=hp)
    imag_part = jnp.einsum("ka,kab->ab", values[:, 1], onehot, precision=hp)
    return complex_block(real_part, imag_part).astype(jnp.bfloat16)


def shards(raw, chirp, steer, offsets, interp, owner):
    tiles = lax.axis_size("tile")
    pulses_here = raw.shape[0]
    channels = raw.shape[1]
    samples = raw.shape[3]
    taps = chirp.shape[2]
    blocks = samples // taps
    span = samples // tiles
    angles = steer.shape[1]
    group_pulses = steer.shape[0]
    split_rows = raw.reshape(pulses_here, channels, 2, blocks, taps)
    table = filter_table(chirp)
    lower_table = table[:, :, :taps]
    upper_table = table[:, :, taps:]
    first_term = jnp.einsum(
        "pcqbu,cquov->pobv", split_rows, lower_table, preferred_element_type=jnp.float32
    )
    second_term = jnp.einsum(
        "pcqbu,cquov->pobv",
        split_rows[:, :, :, 1:],
        upper_table,
        preferred_element_type=jnp.float32,
    )
    second_term = jnp.pad(second_term, ((0, 0), (0, 0), (0, 1), (0, 0)))
    compressed = (first_term + second_term).astype(jnp.bfloat16).reshape(pulses_here, 2, samples)
    scale = 1.0 / math.sqrt(group_pulses)
    cos_part = (jnp.cos(steer) * scale).T.astype(jnp.bfloat16)
    sin_part = (jnp.sin(steer) * scale).T.astype(jnp.bfloat16)
    mine = lax.dynamic_index_in_dim(owner, lax.axis_index("tile"), 0, keepdims=False)
    piece = lax.all_gather(compressed, "tile", axis=0, tiled=True)
    count = piece.shape[0]
    chosen = lax.dynamic_slice_in_dim(piece, mine * span, span, 2)
    stacked = chosen.reshape(2 * count, span)
    weights = steer_block(cos_part, sin_part)
    current = jnp.dot(weights, stacked, preferred_element_type=jnp.float32).astype(jnp.bfloat16)
    levels = lax.axis_size("pulse").bit_length() - 1
    position = lax.axis_index("pulse")
    tap_count = interp.shape[3]
    for level in range(levels):
        half = position // (1 << level) % 2
        level_weights = lax.dynamic_index_in_dim(interp[level], half, 0, keepdims=False)
        own_weights = lax.dynamic_index_in_dim(level_weights, half, 0, keepdims=False)
        other_weights = lax.dynamic_index_in_dim(level_weights, 1 - half, 0, keepdims=False)
        starts = lax.dynamic_index_in_dim(offsets[level], half, 0, keepdims=False)
        targets = starts[None, :, None] + jnp.arange(tap_count, dtype=jnp.int32)[:, None, None]
        onehot = (targets == jnp.arange(angles, dtype=jnp.int32)[None, None, :]).astype(jnp.float32)
        partner = swapped(current, "pulse", level)
        merged = jnp.dot(
            band_matrix(own_weights, onehot), current, preferred_element_type=jnp.float32
        )
        merged = merged + jnp.dot(
            band_matrix(other_weights, onehot), partner, preferred_element_type=jnp.float32
        )
        current = merged.astype(jnp.bfloat16)
    return current.reshape(2, angles, span)


def solution(mesh):
    placed = (P(("pulse", "tile"), None, None, None), P(), P("pulse", None), P(), P(), P())
    return jax.shard_map(
        shards, mesh=mesh, in_specs=placed, out_specs=P(None, "pulse", "tile"), check_vma=False
    )
```

profile of v0, /device:TPU:25, one launch (start us, length us, event | category | flops | bytes accessed | tf_op | source)
XLA Modules:
  0.0 295.0 jit_solution(499325746917621160)
XLA Ops:
  6.5 4.6 %reshape.228 = bf16[16,4,2,64,128,1]{4,3,2,1,0,5:T(8,128)(2,1)} reshape(bf16[16,4,2,8192]{3,2,1,0:T(2,128)(2,1)} %param.6) | data formatting | bytes 4194304 | tf_op jit(solution)/shard_map/reshape | solution.py:64
  11.2 2.8 reshape.203
  14.1 1.3 tile.10
  15.3 0.4 slice.154
  15.7 0.3 reshape.202
  16.1 0.3 copy.17
  16.5 1.1 copy-done.2
  17.6 0.7 fusion.1
  18.4 0.9 copy-done.1
  19.2 0.7 fusion.3
  20.0 0.2 reshape.204
  20.2 1.4 copy.19
  21.8 0.6 dynamic_slice.70
  23.0 0.4 fusion.93
  23.5 0.5 fusion.94
  24.0 0.3 copy.16
  24.4 0.1 copy.40
  24.9 0.1 copy.43
  25.0 0.1 copy.49
  25.2 0.1 copy.51
  29.0 0.3 fusion.144
  29.3 0.3 fusion.146
  29.6 0.3 fusion.142
  29.9 0.3 fusion.148
  30.1 0.3 fusion.140
  30.4 0.3 fusion.143
  30.7 0.3 fusion.145
  31.0 0.3 fusion.141
  31.3 0.3 fusion.147
  31.6 0.3 fusion.139
  31.9 0.3 fusion.149
  32.2 0.3 fusion.150
  32.4 0.3 fusion.137
  32.7 0.3 fusion.138
  33.0 0.3 fusion.151
  33.3 0.3 fusion.152
  33.6 0.5 fusion.135
  34.1 0.3 fusion.136
  34.4 0.3 fusion.153
  34.6 0.3 fusion.154
  34.9 181.8 %all-gather.2.cloned.1.call-done = bf16[256,2,8192]{2,1,0:T(2,128)(2,1)} async-done(((bf16[16,2,8192]{2,1,0:T(2,128)(2,1)}), bf16[256,2,8192]{2,1,0:T(2,128)(2,1)}) %all-gather.2.cloned.1.call-update) | async-done | bytes 8388624 | tf_op jit(solution)/shard_map/all_gather | solution.py:83
  216.8 1.4 constant_dynamic-slice_fusion.5
  218.2 0.2 reshape.205
  218.4 0.3 convolution_convert_fusion
  218.7 2.8 collective-permute-start
  221.6 0.2 fusion.49
  221.8 0.8 collective-permute-done
  222.7 0.2 fusion.4
  222.9 2.2 collective-permute-start.1
  225.2 0.2 fusion.41
  225.4 6.9 %collective-permute-done.1 = bf16[256,512]{1,0:T(8,128)(2,1)S(1)} collective-permute-done((bf16[256,512]{1,0:T(8,128)(2,1)S(1)}, bf16[256,512]{1,0:T(8,128)(2,1)S(1)}, u32[]{:S(2)}, u32[]{:S(2)}) %collective-permute-start.1) | collective-permute-done | bytes 262176 | tf_op jit(solution)/shard_map/ppermute | solution.py:16
  232.3 0.2 fusion.5
  232.5 2.2 collective-permute-start.2
  234.8 0.2 fusion.33
  235.0 14.1 %collective-permute-done.2 = bf16[256,512]{1,0:T(8,128)(2,1)S(1)} collective-permute-done((bf16[256,512]{1,0:T(8,128)(2,1)S(1)}, bf16[256,512]{1,0:T(8,128)(2,1)S(1)}, u32[]{:S(2)}, u32[]{:S(2)}) %collective-permute-start.2) | collective-permute-done | bytes 262176 | tf_op jit(solution)/shard_map/ppermute | solution.py:16
  249.2 0.2 fusion.6
  249.4 3.4 %collective-permute-start.3 = (bf16[256,512]{1,0:T(8,128)(2,1)S(1)}, bf16[256,512]{1,0:T(8,128)(2,1)S(1)}, u32[]{:S(2)}, u32[]{:S(2)}) collective-permute-start(bf16[256,512]{1,0:T(8,128)(2,1)S(1)} %fusion.6), channel_id=1, source_target_pairs={{0,128},{128,0},{16,144},{144,16},{32,160},{160,32},{48,176},{176,... | collective-permute-start | bytes 786440 | tf_op jit(solution)/shard_map/ppermute | solution.py:16
  252.9 0.2 fusion.25
  253.1 14.3 %collective-permute-done.3 = bf16[256,512]{1,0:T(8,128)(2,1)S(1)} collective-permute-done((bf16[256,512]{1,0:T(8,128)(2,1)S(1)}, bf16[256,512]{1,0:T(8,128)(2,1)S(1)}, u32[]{:S(2)}, u32[]{:S(2)}) %collective-permute-start.3) | collective-permute-done | bytes 262176 | tf_op jit(solution)/shard_map/ppermute | solution.py:16
  267.5 0.2 fusion.7
  267.7 4.9 %collective-permute-start.4 = (bf16[256,512]{1,0:T(8,128)(2,1)S(1)}, bf16[256,512]{1,0:T(8,128)(2,1)S(1)}, u32[]{:S(2)}, u32[]{:S(2)}) collective-permute-start(bf16[256,512]{1,0:T(8,128)(2,1)S(1)} %fusion.7), channel_id=1, source_target_pairs={{0,256},{256,0},{16,272},{272,16},{32,288},{288,32},{48,304},{304,... | collective-permute-start | bytes 786440 | tf_op jit(solution)/shard_map/ppermute | solution.py:16
  272.6 0.2 fusion.17
  272.9 14.3 %collective-permute-done.4 = bf16[256,512]{1,0:T(8,128)(2,1)S(1)} collective-permute-done((bf16[256,512]{1,0:T(8,128)(2,1)S(1)}, bf16[256,512]{1,0:T(8,128)(2,1)S(1)}, u32[]{:S(2)}, u32[]{:S(2)}) %collective-permute-start.4) | collective-permute-done | bytes 262176 | tf_op jit(solution)/shard_map/ppermute | solution.py:16
  287.2 0.9 fusion.8
  (121 shorter events, 4.2 us)
Async XLA Ops:
  6.5 4.6 %copy-start = (bf16[16,4,2,8192]{3,2,1,0:T(2,128)(2,1)S(1)}, bf16[16,4,2,8192]{3,2,1,0:T(2,128)(2,1)}, u32[]{:S(2)}) copy-start(bf16[16,4,2,8192]{3,2,1,0:T(2,128)(2,1)} %param.6) | copy-start | bytes 6291460
  6.5 210.2 %all-gather.2.cloned.1.call-start = ((), (), s32[]{:S(2)}) async-start(), calls=%async_computation | async-start | bytes 8912896 | tf_op jit(solution)/shard_map/all_gather | solution.py:83
  11.2 2.8 copy-start.6
  16.0 1.6 copy-start.2
  17.6 1.6 copy-start.1
  19.9 1.8 copy-start.7
  20.0 3.1 %copy-start.3 = (f32[256,128]{1,0:T(8,128)S(1)}, f32[256,128]{1,0:T(8,128)}, u32[]{:S(2)}) copy-start(f32[256,128]{1,0:T(8,128)} %param.8) | copy-start | bytes 393220
  20.2 4.1 %copy-start.4 = (bf16[5,2,2,4,2,128]{5,4,3,2,1,0:T(2,128)(2,1)S(1)}, bf16[5,2,2,4,2,128]{5,4,3,2,1,0:T(2,128)(2,1)}, u32[]{:S(2)}) copy-start(bf16[5,2,2,4,2,128]{5,4,3,2,1,0:T(2,128)(2,1)} %param.10) | copy-start | bytes 122884
  20.2 4.4 %copy-start.5 = (s32[5,2,128]{2,1,0:T(2,128)S(1)}, s32[5,2,128]{2,1,0:T(2,128)}, u32[]{:S(2)}) copy-start(s32[5,2,128]{2,1,0:T(2,128)} %param.9) | copy-start | bytes 15364
  218.7 4.0 %collective-permute-start = (bf16[256,512]{1,0:T(8,128)(2,1)S(1)}, bf16[256,512]{1,0:T(8,128)(2,1)S(1)}, u32[]{:S(2)}, u32[]{:S(2)}) collective-permute-start(bf16[256,512]{1,0:T(8,128)(2,1)S(1)} %convolution_convert_fusion), channel_id=1, source_target_pairs={{0,16},{16,0},{32,48},{48,32},{64,80},{80,64},{96,112},{112,96},{1... | collective-permute-start | bytes 786440 | tf_op jit(solution)/shard_map/ppermute | solution.py:16
  222.9 9.4 %collective-permute-start.1 = (bf16[256,512]{1,0:T(8,128)(2,1)S(1)}, bf16[256,512]{1,0:T(8,128)(2,1)S(1)}, u32[]{:S(2)}, u32[]{:S(2)}) collective-permute-start(bf16[256,512]{1,0:T(8,128)(2,1)S(1)} %fusion.4), channel_id=1, source_target_pairs={{0,32},{32,0},{16,48},{48,16},{64,96},{96,64},{80,112},{112,80},{1... | collective-permute-start | bytes 786440 | tf_op jit(solution)/shard_map/ppermute | solution.py:16
  232.5 16.6 %collective-permute-start.2 = (bf16[256,512]{1,0:T(8,128)(2,1)S(1)}, bf16[256,512]{1,0:T(8,128)(2,1)S(1)}, u32[]{:S(2)}, u32[]{:S(2)}) collective-permute-start(bf16[256,512]{1,0:T(8,128)(2,1)S(1)} %fusion.5), channel_id=1, source_target_pairs={{0,64},{64,0},{16,80},{80,16},{32,96},{96,32},{48,112},{112,48},{1... | collective-permute-start | bytes 786440 | tf_op jit(solution)/shard_map/ppermute | solution.py:16
  249.4 18.1 %collective-permute-start.3 = (bf16[256,512]{1,0:T(8,128)(2,1)S(1)}, bf16[256,512]{1,0:T(8,128)(2,1)S(1)}, u32[]{:S(2)}, u32[]{:S(2)}) collective-permute-start(bf16[256,512]{1,0:T(8,128)(2,1)S(1)} %fusion.6), channel_id=1, source_target_pairs={{0,128},{128,0},{16,144},{144,16},{32,160},{160,32},{48,176},{176,... | collective-permute-start | bytes 786440 | tf_op jit(solution)/shard_map/ppermute | solution.py:16
  267.7 19.5 %collective-permute-start.4 = (bf16[256,512]{1,0:T(8,128)(2,1)S(1)}, bf16[256,512]{1,0:T(8,128)(2,1)S(1)}, u32[]{:S(2)}, u32[]{:S(2)}) collective-permute-start(bf16[256,512]{1,0:T(8,128)(2,1)S(1)} %fusion.7), channel_id=1, source_target_pairs={{0,256},{256,0},{16,272},{272,16},{32,288},{288,32},{48,304},{304,... | collective-permute-start | bytes 786440 | tf_op jit(solution)/shard_map/ppermute | solution.py:16
Sparse Core Ops, SparseCore 0:
  21.8 194.9 all-gather.1
where the time goes:
time: 295 us
  waiting for transfers between devices  232 us (79%)
  local copies, waits for them, and re-layouts  19.4 us (7%)
  starting transfers between devices  15.4 us (5%)
  between operations  15.3 us (5%)
  matrix products  10.4 us (4%)
    all_gather x1, waiting for transfers between devices, shards(): piece = lax.all_gather(compressed, 'tile', axis=0, tiled=True)  182 us
    ppermute x5, waiting for transfers between devices, swapped(): return lax.ppermute(block, axis, route)  50.6 us
    ppermute x5, starting transfers between devices, swapped(): return lax.ppermute(block, axis, route)  15.4 us
    reshape x2, local copies, waits for them, and re-layouts, shards(): split_rows = raw.reshape(pulses_here, channels, 2, blocks, taps)  7.43 us
  transfers between devices with their start and end apart: 6, of which 6 were waited for; matrix products, arithmetic and copies ran while one was open for 4% of the time, Pallas kernels for 0%

commit v1 on v0

v1 whole, which is shorter than its diff:
```python
import functools
import itertools
import math

import jax
import jax.numpy as jnp
import numpy as np
from jax import lax
from jax.experimental import pallas as pl
from jax.experimental.pallas import tpu as pltpu
from jax.sharding import Mesh
from jax.sharding import PartitionSpec as P

S = 8192
CH = 4
KTAP = 128
A = 128
KB = 4
R = 512
P_G = 256
N_TILE = 16
P_HERE = 16
BLOCKS = S // KTAP
PER = R // KTAP
WIN = 20
HALF = 80
N_FAR = 16
F32 = jnp.float32
BF16 = jnp.bfloat16
VMEM = pl.BlockSpec(memory_space=pltpu.VMEM)
SMEM = pl.BlockSpec(memory_space=pltpu.SMEM)


def band_range(half, low, high):
    first = min(max((half * A + low) // 2 - KB // 2, 0), A - KB)
    last = min(max((half * A + high) // 2, 0), A - KB)
    return first, last + KB - 1


def far_window(bits):
    low, high = 0, A - 1
    for half in reversed(bits):
        low, high = band_range(half, low, high)
    return low, high


def far_lows():
    lows = []
    for d in range(N_FAR):
        low, high = far_window([d >> i & 1 for i in range(4)])
        assert high - low + 1 <= WIN
        lows.append(low)
    return lows


def row_pick():
    table = np.zeros((N_FAR, 2, WIN, 2, A), np.float32)
    for d, low in enumerate(far_lows()):
        for part in range(2):
            for i in range(WIN):
                if low + i < A:
                    table[d, part, i, part, low + i] = 1
    return table.reshape(N_FAR * 2 * WIN, 2 * A).astype(jnp.bfloat16)


def order_pick():
    table = np.zeros((2, 8, P_HERE, P_HERE, 8, 2), np.float32)
    for q, b, p in itertools.product(range(2), range(8), range(P_HERE)):
        table[q, b, p, p, b, q] = 1
    return table.reshape(256, 256).astype(jnp.bfloat16)


def compress_kernel(owner_ref, chirp_ref, pick_ref, x_ref, out_ref, inv_ref, table_ref, z_ref):
    for t in range(N_TILE):
        inv_ref[owner_ref[t]] = t
    row = lax.broadcasted_iota(jnp.int32, (KTAP, KTAP), 0)
    col = lax.broadcasted_iota(jnp.int32, (KTAP, KTAP), 1)
    flip = jnp.where((row + col) % KTAP == 0, 1.0, 0.0).astype(BF16)
    half = CH * KTAP
    for c in range(CH):
        taps = chirp_ref[c].astype(F32)
        for q in range(2):
            line = jnp.broadcast_to(taps[q : q + 1], (16, KTAP)).astype(BF16)
            line = jnp.dot(line, flip, preferred_element_type=F32)
            circ = jnp.broadcast_to(line[0:1], (KTAP, KTAP))
            circ = pltpu.roll(circ, 0, 1, stride=1, stride_axis=0)
            for upper in range(2):
                keep = (row < col) if upper else (row >= col)
                kept = jnp.where(keep, circ, 0.0)
                base = upper * 2 * half + c * KTAP
                if q == 0:
                    table_ref[base : base + KTAP, 0:KTAP] = kept.astype(BF16)
                    table_ref[base + half : base + half + KTAP, KTAP:] = kept.astype(BF16)
                else:
                    table_ref[base : base + KTAP, KTAP:] = kept.astype(BF16)
                    table_ref[base + half : base + half + KTAP, 0:KTAP] = (-kept).astype(BF16)
    z_ref[BLOCKS * P_HERE :, :] = jnp.zeros((P_HERE, 2 * half), BF16)
    pick = pick_ref[...]
    for g in range(BLOCKS // 8):
        parts = []
        for c in range(CH):
            got = x_ref[:, c, 16 * g : 16 * g + 16, :]
            parts.append(got.reshape(256, KTAP))
        moved = jnp.dot(pick, jnp.concatenate(parts, axis=1), preferred_element_type=F32)
        moved = moved.astype(BF16)
        z_ref[128 * g : 128 * g + 128, 0:half] = moved[0:128]
        z_ref[128 * g : 128 * g + 128, half:] = moved[128:256]
    for m in range(4):
        lower = z_ref[256 * m : 256 * m + 256, :]
        upper = z_ref[256 * m + 16 : 256 * m + 272, :]
        acc = jnp.dot(lower, table_ref[0 : 2 * half, :], preferred_element_type=F32)
        acc = acc + jnp.dot(upper, table_ref[2 * half :, :], preferred_element_type=F32)
        acc = acc.astype(BF16)
        for n in range(4):
            to = inv_ref[4 * m + n]
            for j in range(PER):
                base = 16 * (PER * n + j)
                for o in range(2):
                    out_ref[to, j, o] = acc[base : base + 16, 128 * o : 128 * o + 128]


def project_kernel(pos_ref, steer_ref, got_ref, send_ref, own_ref, w_ref):
    theta = steer_ref[...]
    scale = 1.0 / math.sqrt(P_G)
    cos_part = (jnp.cos(theta) * scale).astype(BF16).reshape(N_TILE, P_HERE, A)
    sin_part = (jnp.sin(theta) * scale).astype(BF16).reshape(N_TILE, P_HERE, A)
    first = jnp.concatenate([cos_part, sin_part], axis=2)
    second = jnp.concatenate([-sin_part, cos_part], axis=2)
    full = jnp.stack([first, second], axis=1).reshape(2 * P_G, 2 * A)
    w_ref[...] = full.T
    mine = pos_ref[0]
    rows = []
    for half in (1 - mine, mine):
        low = pl.multiple_of(half * (A - HALF), 16)
        rows.append(w_ref[pl.ds(low, HALF), :])
        rows.append(w_ref[pl.ds(pl.multiple_of(A + low, 16), HALF), :])
    weights = jnp.concatenate(rows, axis=0)
    for j in range(PER):
        block = got_ref[:, 32 * j : 32 * j + 32, :].reshape(2 * P_G, KTAP)
        made = jnp.dot(weights, block, preferred_element_type=F32).astype(BF16)
        send_ref[:, 128 * j : 128 * j + 128] = made[: 2 * HALF]
        own_ref[:, 128 * j : 128 * j + 128] = made[2 * HALF :]


def band_t(interp_ref, offsets_ref, level, half, child, low, count):
    both = offsets_ref[level]
    starts = jnp.where(half == 0, both[0:1], both[1:2])
    row = lax.broadcasted_iota(jnp.int32, (count, A), 0) + low
    delta = row - starts
    real = jnp.zeros((count, A), F32)
    imag = jnp.zeros((count, A), F32)
    for k in range(KB):
        taps = interp_ref[level, half, child, k].astype(F32)
        hit = delta == k
        real = jnp.where(hit, taps[0:1], real)
        imag = jnp.where(hit, taps[1:2], imag)
    upper = jnp.concatenate([real, imag], axis=1)
    lower = jnp.concatenate([-imag, real], axis=1)
    return jnp.concatenate([upper, lower], axis=0).astype(BF16)


def tables_kernel(pos_ref, lows_ref, interp_ref, offsets_ref, pick_ref, near_ref, far_ref):
    nt = (((1,), (1,)), ((), ()))
    mine = pos_ref[0]
    d = pos_ref[1]
    low = mine * (A - HALF)
    near = [
        band_t(interp_ref, offsets_ref, 0, mine, mine, low, HALF),
        band_t(interp_ref, offsets_ref, 0, mine, 1 - mine, low, HALF),
    ]
    near = jnp.concatenate(near, axis=0)
    near_ref[...] = lax.dot_general(pick_ref[...], near, nt, preferred_element_type=F32).astype(BF16)
    bits = [d & 1, d // 2 & 1, d // 4 & 1, d // 8 & 1]
    low = lows_ref[d]
    stack = [band_t(interp_ref, offsets_ref, 1, bits[0], q, low, WIN) for q in range(2)]
    chain = jnp.concatenate(stack, axis=0)
    for level in range(2, 5):
        grown = []
        for q in range(2):
            step = band_t(interp_ref, offsets_ref, level, bits[level - 1], q, 0, A)
            grown.append(jnp.dot(chain, step, preferred_element_type=F32).astype(BF16))
        chain = jnp.concatenate(grown, axis=0)
    far_ref[...] = chain.T


def merge_kernel(near_ref, own_ref, other_ref, out_ref):
    data = jnp.concatenate([own_ref[...], other_ref[...]], axis=0)
    made = jnp.dot(near_ref[...], data, preferred_element_type=F32)
    made = made.astype(BF16)
    for d in range(N_FAR):
        for j in range(PER):
            out_ref[d, j] = made[2 * WIN * d : 2 * WIN * d + 2 * WIN, 128 * j : 128 * j + 128]


def final_kernel(far_ref, got_ref, out_ref):
    for j in range(PER):
        block = got_ref[:, j].reshape(N_FAR * 2 * WIN, KTAP)
        made = jnp.dot(far_ref[...], block, preferred_element_type=F32).astype(BF16)
        out_ref[0, :, 128 * j : 128 * j + 128] = made[:A]
        out_ref[1, :, 128 * j : 128 * j + 128] = made[A:]


def call(body, ins, outs, scratch=(), limit=48):
    return pl.pallas_call(
        body,
        out_shape=[jax.ShapeDtypeStruct(shape, BF16) for shape in outs],
        in_specs=ins,
        out_specs=[VMEM] * len(outs),
        scratch_shapes=list(scratch),
        compiler_params=pltpu.CompilerParams(vmem_limit_bytes=limit * 2**20),
    )


def shards(raw, chirp, steer, offsets, interp, owner):
    mine = lax.axis_index("c")
    far = lax.axis_index("h") * 8 + lax.axis_index("y")
    pos = jnp.stack([mine, far]).astype(jnp.int32)
    x = raw.reshape(P_HERE, CH, 2, BLOCKS, KTAP).transpose(0, 1, 3, 2, 4)
    x = x.reshape(P_HERE, CH, 2 * BLOCKS, KTAP)
    (packed,) = call(
        compress_kernel,
        [SMEM, VMEM, VMEM, VMEM],
        [(N_TILE, PER, 2, P_HERE, KTAP)],
        [
            pltpu.SMEM((N_TILE,), jnp.int32),
            pltpu.VMEM((4 * CH * KTAP, 2 * KTAP), BF16),
            pltpu.VMEM(((BLOCKS + 1) * P_HERE, 2 * CH * KTAP), BF16),
        ],
    )(owner, chirp, jnp.asarray(order_pick()), x)
    packed = packed.reshape(N_TILE, PER * 2 * P_HERE, KTAP)
    got = lax.all_to_all(packed, ("x", "l"), 0, 0, tiled=True)
    near, far_table = call(
        tables_kernel,
        [SMEM, SMEM, VMEM, VMEM, VMEM],
        [(N_FAR * 2 * WIN, 4 * HALF), (2 * A, N_FAR * 2 * WIN)],
    )(pos, jnp.asarray(far_lows(), jnp.int32), interp, offsets, jnp.asarray(row_pick()))
    send, own = call(
        project_kernel,
        [SMEM, VMEM, VMEM],
        [(2 * HALF, R), (2 * HALF, R)],
        [pltpu.VMEM((2 * A, 2 * P_G), BF16)],
    )(pos, steer, got)
    other = lax.ppermute(send, "c", [(0, 1), (1, 0)])
    (pieces,) = call(merge_kernel, [VMEM] * 3, [(N_FAR, PER, 2 * WIN, KTAP)])(near, own, other)
    pieces = pieces.reshape(N_FAR, PER * 2 * WIN, KTAP)
    parts = lax.all_to_all(pieces, ("h", "y"), 0, 0, tiled=True)
    parts = parts.reshape(N_FAR, PER, 2 * WIN, KTAP)
    (image,) = call(final_kernel, [VMEM] * 2, [(2, A, R)])(far_table, parts)
    return image


def solution(mesh):
    split = Mesh(mesh.devices.reshape(2, 8, 2, 4, 4), ("h", "y", "c", "x", "l"))
    pulse = ("h", "y", "c")
    tile = ("x", "l")
    placed = (P(pulse + tile, None, None, None), P(), P(pulse, None), P(), P(), P())
    return jax.shard_map(
        shards, mesh=split, in_specs=placed, out_specs=P(None, pulse, tile), check_vma=False
    )
```

time: 295 us -> 77.3 us (0.26)
  the two profiles are of different devices: /device:TPU:25 before, /device:TPU:8 now
where the time goes in v1:
time: 77.3 us; the launch traced here: 76.9 us
  blocking collectives  36.9 us (48%)
  waiting for transfers between devices  16.4 us (21%)
  starting transfers between devices  11.7 us (15%)
  Pallas kernels  7.83 us (10%)
  local copies, waits for them, and re-layouts  3.85 us (5%)
    all_to_all x1, blocking collectives, shards(): parts = lax.all_to_all(pieces, ('h', 'y'), 0, 0, tiled=True)  36.9 us
    all_to_all x1, waiting for transfers between devices, shards(): got = lax.all_to_all(packed, ('x', 'l'), 0, 0, tiled=True)  16.4 us
    all_to_all x1, starting transfers between devices, shards(): got = lax.all_to_all(packed, ('x', 'l'), 0, 0, tiled=True)  9.82 us
    unnamed x18, local copies, waits for them, and re-layouts  3.85 us
    pallas_call x1, Pallas kernels, shards(): call(compress_kernel, [SMEM, VMEM, VMEM, VMEM], [(N_TILE, PER, 2, P_HERE,...  3.27 us
    ppermute x1, starting transfers between devices, shards(): other = lax.ppermute(send, 'c', [(0, 1), (1, 0)])  1.92 us
  transfers between devices with their start and end apart: 2, of which 1 were waited for; matrix products, arithmetic and copies ran while one was open for 0% of the time, Pallas kernels for 2%

profile of v1, /device:TPU:8, one launch (start us, length us, event | category | flops | bytes accessed | tf_op | source)
XLA Modules:
  0.0 76.9 jit_solution(3443796429998991720)
XLA Ops:
  0.0 0.0 copy-start
  0.0 1.6 %copy-done = bf16[16,4,2,8192]{3,2,1,0:T(2,128)(2,1)S(1)} copy-done((bf16[16,4,2,8192]{3,2,1,0:T(2,128)(2,1)S(1)}, bf16[16,4,2,8192]{3,2,1,0:T(2,128)(2,1)}, u32[]{:S(2)}) %copy-start) | copy-done | bytes 2097176
  1.6 0.0 copy-start.3
  1.6 0.9 %copy-done.3 = bf16[256,256]{1,0:T(8,128)(2,1)S(1)} copy-done((bf16[256,256]{1,0:T(8,128)(2,1)S(1)}, bf16[256,256]{1,0:T(8,128)(2,1)}, u32[]{:S(2)}) %copy-start.3) | copy-done | bytes 131096
  2.5 0.0 copy-start.6
  2.5 0.7 copy-done.6
  3.2 0.0 copy-start.8
  3.2 0.7 copy-done.8
  3.8 0.0 copy-start.2
  3.8 0.0 copy-start.1
  3.8 0.0 copy-start.4
  3.8 0.0 copy-start.5
  3.8 0.0 copy-start.7
  3.9 3.3 %shard_map.92 = bf16[16,4,2,16,128]{4,3,2,1,0:T(8,128)(2,1)} custom-call(s32[16]{0:T(128)S(1)} %copy-done.8, bf16[4,2,128]{2,1,0:T(2,128)(2,1)S(1)} %copy-done.6, bf16[256,256]{1,0:T(8,128)(2,1)S(1)} %copy-done.3, bf16[16,4,128,128]{3,2,1,0:T(8,128)(2,1)S(1)} %bitcast.12), custom_call_target="tpu_custom_call" | custom-call | tf_op jit(solution)/shard_map/pallas_call | solution.py:220
  7.1 9.8 %all-to-all-start = ((bf16[16,128,128]{2,1,0:T(8,128)(2,1)}), bf16[16,128,128]{2,1,0:T(8,128)(2,1)S(1)}, u32[]{:S(2)}, u32[]{:S(2)}) async-start(bf16[16,128,128]{2,1,0:T(8,128)(2,1)} %bitcast.5), calls=%async_computation | async-start | bytes 1048576 | tf_op jit(solution)/shard_map/all_to_all | solution.py:231
  17.0 0.1 pad_add_fusion.pos_ref
  17.0 16.4 %all-to-all-done.got_ref = bf16[16,128,128]{2,1,0:T(8,128)(2,1)S(1)} async-done(((bf16[16,128,128]{2,1,0:T(8,128)(2,1)}), bf16[16,128,128]{2,1,0:T(8,128)(2,1)S(1)}, u32[]{:S(2)}, u32[]{:S(2)}) %all-to-all-start) | async-done | bytes 524320 | tf_op jit(solution)/shard_map/all_to_all | solution.py:231
  33.5 0.0 copy-done.2
  33.5 1.5 %shard_map.93 = (bf16[160,512]{1,0:T(8,128)(2,1)S(1)}, bf16[160,512]{1,0:T(8,128)(2,1)S(1)}) custom-call(s32[2]{0:T(128)S(1)} %pad_add_fusion.pos_ref, f32[256,128]{1,0:T(8,128)S(1)} %copy-done.2, bf16[16,128,128]{2,1,0:T(8,128)(2,1)S(1)} %all-to-all-done.got_ref), custom_call_target="tpu_custom_call" | custom-call | tf_op jit(solution)/shard_map/pallas_call | solution.py:237
  35.0 1.9 %collective-permute-start = (bf16[160,512]{1,0:T(8,128)(2,1)S(1)}, bf16[160,512]{1,0:T(8,128)(2,1)S(1)}, u32[]{:S(2)}, u32[]{:S(2)}) collective-permute-start(bf16[160,512]{1,0:T(8,128)(2,1)S(1)} %get-tuple-element.12), channel_id=1, source_target_pairs={{0,16},{16,0},{1,17},{17,1},{2,18},{18,2},{3,19},{19,3},{4,20},{20... | collective-permute-start | bytes 491528 | tf_op jit(solution)/shard_map/ppermute | solution.py:243
  37.0 0.0 copy-done.1
  37.0 0.0 copy-done.4
  37.0 0.0 copy-done.5
  37.0 0.0 copy-done.7
  37.0 1.3 %shard_map.91 = (bf16[640,320]{1,0:T(8,128)(2,1)S(1)}, bf16[256,640]{1,0:T(8,128)(2,1)S(1)}) custom-call(s32[2]{0:T(128)S(1)} %pad_add_fusion.pos_ref, s32[16]{0:T(128)S(1)} %copy-done.7, bf16[5,2,2,4,2,128]{5,4,3,2,1,0:T(2,128)(2,1)S(1)} %copy-done.4, s32[5,2,128]{2,1,0:T(2,128)S(1)} %copy-done.5, bf16[640,256]{1,0:T(8,128)(2,1)S(1)} %copy-done.1), custom_call_target="tpu_custom_call" | custom-call | tf_op jit(solution)/shard_map/pallas_call | solution.py:232
  38.3 0.0 collective-permute-done.other_ref
  38.3 0.5 shard_map.94
  38.8 36.9 %all_to_all.10 = bf16[16,160,128]{2,1,0:T(8,128)(2,1)S(1)} all-to-all(bf16[16,160,128]{2,1,0:T(8,128)(2,1)S(1)} %bitcast.10), channel_id=1, replica_groups=mesh['h'=2,'y'=8,'c'=2,'x'=4,'l'=4] {'h','y'}, dimensions={0} | all-to-all | bytes 1310720 | tf_op jit(solution)/shard_map/all_to_all | solution.py:246
  75.7 1.2 %shard_map.95 = bf16[2,128,512]{2,1,0:T(8,128)(2,1)} custom-call(bf16[256,640]{1,0:T(8,128)(2,1)S(1)} %get-tuple-element.9.far_ref, bf16[16,4,40,128]{3,2,1,0:T(8,128)(2,1)S(1)} %bitcast.11), custom_call_target="tpu_custom_call" | custom-call | tf_op jit(solution)/shard_map/pallas_call | solution.py:248
Async XLA Ops:
  0.0 1.6 %copy-start = (bf16[16,4,2,8192]{3,2,1,0:T(2,128)(2,1)S(1)}, bf16[16,4,2,8192]{3,2,1,0:T(2,128)(2,1)}, u32[]{:S(2)}) copy-start(bf16[16,4,2,8192]{3,2,1,0:T(2,128)(2,1)} %param.9) | copy-start | bytes 6291460
  1.6 0.9 %copy-start.3 = (bf16[256,256]{1,0:T(8,128)(2,1)S(1)}, bf16[256,256]{1,0:T(8,128)(2,1)}, u32[]{:S(2)}) copy-start(bf16[256,256]{1,0:T(8,128)(2,1)} %constant.24.clone.pick_ref) | copy-start | bytes 393220
  2.5 0.7 copy-start.6
  3.2 0.7 copy-start.8
  3.8 29.6 %copy-start.2 = (f32[256,128]{1,0:T(8,128)S(1)}, f32[256,128]{1,0:T(8,128)}, u32[]{:S(2)}) copy-start(f32[256,128]{1,0:T(8,128)} %steer_ref.1) | copy-start | bytes 393220
  3.8 33.1 %copy-start.1 = (bf16[640,256]{1,0:T(8,128)(2,1)S(1)}, bf16[640,256]{1,0:T(8,128)(2,1)}, u32[]{:S(2)}) copy-start(bf16[640,256]{1,0:T(8,128)(2,1)} %constant.26.clone.pick_ref) | copy-start | bytes 983044
  3.8 33.1 %copy-start.4 = (bf16[5,2,2,4,2,128]{5,4,3,2,1,0:T(2,128)(2,1)S(1)}, bf16[5,2,2,4,2,128]{5,4,3,2,1,0:T(2,128)(2,1)}, u32[]{:S(2)}) copy-start(bf16[5,2,2,4,2,128]{5,4,3,2,1,0:T(2,128)(2,1)} %interp_ref.1) | copy-start | bytes 122884
  3.8 33.1 %copy-start.5 = (s32[5,2,128]{2,1,0:T(2,128)S(1)}, s32[5,2,128]{2,1,0:T(2,128)}, u32[]{:S(2)}) copy-start(s32[5,2,128]{2,1,0:T(2,128)} %offsets_ref.1) | copy-start | bytes 15364
  3.8 33.1 %copy-start.7 = (s32[16]{0:T(128)S(1)}, s32[16]{0:T(128)}, u32[]{:S(2)}) copy-start(s32[16]{0:T(128)} %constant.25.clone.lows_ref) | copy-start | bytes 196
  7.1 26.3 %all-to-all-start = ((bf16[16,128,128]{2,1,0:T(8,128)(2,1)}), bf16[16,128,128]{2,1,0:T(8,128)(2,1)S(1)}, u32[]{:S(2)}, u32[]{:S(2)}) async-start(bf16[16,128,128]{2,1,0:T(8,128)(2,1)} %bitcast.5), calls=%async_computation | async-start | bytes 1048576 | tf_op jit(solution)/shard_map/all_to_all | solution.py:231
  35.0 3.3 %collective-permute-start = (bf16[160,512]{1,0:T(8,128)(2,1)S(1)}, bf16[160,512]{1,0:T(8,128)(2,1)S(1)}, u32[]{:S(2)}, u32[]{:S(2)}) collective-permute-start(bf16[160,512]{1,0:T(8,128)(2,1)S(1)} %get-tuple-element.12), channel_id=1, source_target_pairs={{0,16},{16,0},{1,17},{17,1},{2,18},{18,2},{3,19},{19,3},{4,20},{20... | collective-permute-start | bytes 491528 | tf_op jit(solution)/shard_map/ppermute | solution.py:243

commit v2 on v1

v2 whole, which is shorter than its diff:
```python
import math

import jax
import jax.numpy as jnp
import numpy as np
from jax import lax
from jax.experimental import pallas as pl
from jax.experimental.pallas import tpu as pltpu
from jax.sharding import Mesh
from jax.sharding import PartitionSpec as P

S = 8192
CH = 4
KTAP = 128
A = 128
KB = 4
R = 512
P_G = 256
N_TILE = 16
P_HERE = 16
BLOCKS = S // KTAP
PER = R // KTAP
WIN = 25
MAIN = 48
REST = 4
FAR_ROWS = 56
PIECE = PER * (MAIN + REST)
HALF = 72
N_Y = 8
F32 = jnp.float32
BF16 = jnp.bfloat16
VMEM = pl.BlockSpec(memory_space=pltpu.VMEM)
HBM = pl.BlockSpec(memory_space=pltpu.HBM)


def band_range(half, low, high):
    first = min(max((half * A + low) // 2 - KB // 2, 0), A - KB)
    last = min(max((half * A + high) // 2, 0), A - KB)
    return first, last + KB - 1


def window_lows():
    lows = []
    for y in range(N_Y):
        low, high = 0, A - 1
        for level in (3, 2, 1):
            low, high = band_range(y >> level - 1 & 1, low, high)
        assert high - low + 1 <= WIN
        lows.append(low)
    return lows


def row_pick():
    table = np.zeros((N_Y, MAIN + REST, 2, A), np.float32)
    for y, low in enumerate(window_lows()):
        for part in range(2):
            for i in range(min(WIN, A - low)):
                table[y, part * WIN + i, part, low + i] = 1
    table = table.reshape(N_Y, MAIN + REST, 2 * A)
    first = table[:, :MAIN].reshape(N_Y * MAIN, 2 * A)
    rest = table[:, MAIN:].reshape(N_Y * REST, 2 * A)
    return np.concatenate([first, rest]).astype(jnp.bfloat16)


def one_hot(rows, cols, wanted):
    row = lax.broadcasted_iota(jnp.int32, (rows, cols), 0)
    col = lax.broadcasted_iota(jnp.int32, (rows, cols), 1)
    return jnp.where(wanted(row, col), 1.0, 0.0).astype(BF16)


def compress_kernel(
    owner_hbm, chirp_hbm, x_hbm, out_ref, token_ref, owner_ref, chirp_ref, x_ref, inv_ref, table_ref, z_ref, sem
):
    steps = BLOCKS // 8
    loads = [
        pltpu.make_async_copy(
            x_hbm.at[:, :, 16 * g : 16 * g + 16, :], x_ref.at[:, :, 16 * g : 16 * g + 16, :], sem.at[g]
        )
        for g in range(steps)
    ]
    chirp_load = pltpu.make_async_copy(chirp_hbm, chirp_ref, sem.at[steps])
    owner_load = pltpu.make_async_copy(owner_hbm, owner_ref, sem.at[steps + 1])
    token_ref[...] = jnp.zeros(token_ref.shape, BF16)
    chirp_load.start()
    for load in loads:
        load.start()
    owner_load.start()
    row = lax.broadcasted_iota(jnp.int32, (KTAP, KTAP), 0)
    col = lax.broadcasted_iota(jnp.int32, (KTAP, KTAP), 1)
    flip = jnp.where((row + col) % KTAP == 0, 1.0, 0.0).astype(BF16)
    pick = one_hot(256, 256, lambda r, c: c == r % 16 * 16 + r // 16 % 8 * 2 + r // 128)
    half = CH * KTAP
    z_ref[BLOCKS * P_HERE :, :] = jnp.zeros((P_HERE, 2 * half), BF16)
    chirp_load.wait()
    for c in range(CH):
        taps = chirp_ref[c].astype(F32)
        for q in range(2):
            line = jnp.broadcast_to(taps[q : q + 1], (16, KTAP)).astype(BF16)
            line = jnp.dot(line, flip, preferred_element_type=F32)
            circ = jnp.broadcast_to(line[0:1], (KTAP, KTAP))
            circ = pltpu.roll(circ, 0, 1, stride=1, stride_axis=0)
            for upper in range(2):
                keep = (row < col) if upper else (row >= col)
                kept = jnp.where(keep, circ, 0.0)
                base = upper * 2 * half + c * KTAP
                if q == 0:
                    table_ref[base : base + KTAP, 0:KTAP] = kept.astype(BF16)
                    table_ref[base + half : base + half + KTAP, KTAP:] = kept.astype(BF16)
                else:
                    table_ref[base : base + KTAP, KTAP:] = kept.astype(BF16)
                    table_ref[base + half : base + half + KTAP, 0:KTAP] = (-kept).astype(BF16)
    owner_load.wait()
    for t in range(N_TILE):
        inv_ref[owner_ref[t]] = t
    for g in range(steps):
        loads[g].wait()
        parts = []
        for c in range(CH):
            got = x_ref[:, c, 16 * g : 16 * g + 16, :]
            parts.append(got.reshape(256, KTAP))
        moved = jnp.dot(pick, jnp.concatenate(parts, axis=1), preferred_element_type=F32)
        moved = moved.astype(BF16)
        z_ref[128 * g : 128 * g + 128, 0:half] = moved[0:128]
        z_ref[128 * g : 128 * g + 128, half:] = moved[128:256]
    for m in range(4):
        lower = z_ref[256 * m : 256 * m + 256, :]
        upper = z_ref[256 * m + 16 : 256 * m + 272, :]
        acc = jnp.dot(lower, table_ref[0 : 2 * half, :], preferred_element_type=F32)
        acc = acc + jnp.dot(upper, table_ref[2 * half :, :], preferred_element_type=F32)
        acc = acc.astype(BF16)
        for n in range(4):
            to = inv_ref[4 * m + n]
            for j in range(PER):
                base = 16 * (PER * n + j)
                for o in range(2):
                    out_ref[to, j, o] = acc[base : base + 16, 128 * o : 128 * o + 128]


def band_parts(interp_ref, offsets_ref, level, half, child, rows):
    both = offsets_ref[level]
    starts = jnp.where(half == 0, both[0:1], both[1:2])
    delta = rows - starts
    real = jnp.zeros(rows.shape, F32)
    imag = jnp.zeros(rows.shape, F32)
    for k in range(KB):
        taps = interp_ref[level, half, child, k].astype(F32)
        hit = delta == k
        real = jnp.where(hit, taps[0:1], real)
        imag = jnp.where(hit, taps[1:2], imag)
    return real, imag


def band_t(interp_ref, offsets_ref, level, half, child, low, count):
    rows = lax.broadcasted_iota(jnp.int32, (count, A), 0) + low
    real, imag = band_parts(interp_ref, offsets_ref, level, half, child, rows)
    upper = jnp.concatenate([real, imag], axis=1)
    lower = jnp.concatenate([-imag, real], axis=1)
    return jnp.concatenate([upper, lower], axis=0).astype(BF16)


def prep_kernel(after_ref, steer_ref, interp_ref, offsets_ref, pick_ref, weights_ref, near_ref, w_ref):
    del after_ref
    mine = lax.axis_index("c")
    theta = steer_ref[...]
    scale = 1.0 / math.sqrt(P_G)
    cos_part = (jnp.cos(theta) * scale).astype(BF16).reshape(N_TILE, P_HERE, A)
    sin_part = (jnp.sin(theta) * scale).astype(BF16).reshape(N_TILE, P_HERE, A)
    first = jnp.concatenate([cos_part, sin_part], axis=2)
    second = jnp.concatenate([-sin_part, cos_part], axis=2)
    full = jnp.stack([first, second], axis=1).reshape(2 * P_G, 2 * A)
    w_ref[...] = full.T.astype(F32)
    half_rows(w_ref, weights_ref, mine)
    low = mine * (A - HALF)
    near = [
        band_t(interp_ref, offsets_ref, 0, mine, mine, low, HALF),
        band_t(interp_ref, offsets_ref, 0, mine, 1 - mine, low, HALF),
    ]
    near = jnp.concatenate(near, axis=0)
    nt = (((1,), (1,)), ((), ()))
    near_ref[...] = lax.dot_general(pick_ref[...], near, nt, preferred_element_type=F32).astype(BF16)


def half_rows(full_ref, out_ref, mine):
    for n, side in enumerate((1 - mine, mine)):
        for part in range(2):
            low = pl.multiple_of(part * A + side * (A - HALF), 8)
            at = (2 * n + part) * HALF
            out_ref[at : at + HALF, :] = full_ref[pl.ds(low, HALF), :].astype(BF16)


def project_kernel(weights_ref, got_ref, send_ref, own_ref):
    for j in range(PER):
        block = got_ref[:, 32 * j : 32 * j + 32, :].reshape(2 * P_G, KTAP)
        made = jnp.dot(weights_ref[...], block, preferred_element_type=F32).astype(BF16)
        send_ref[:, 128 * j : 128 * j + 128] = made[: 2 * HALF]
        own_ref[:, 128 * j : 128 * j + 128] = made[2 * HALF :]


def far_kernel(after_ref, interp_ref, offsets_ref, far_ref, full_ref):
    del after_ref
    y = lax.axis_index("y")
    bits = [y & 1, y >> 1 & 1, y >> 2 & 1]
    low = jnp.int32(0)
    for bit in reversed(bits):
        low = jnp.clip((bit * A + low) // 2 - KB // 2, 0, A - KB)
    n = lax.broadcasted_iota(jnp.int32, (FAR_ROWS, A), 0)
    second = n >= WIN
    rows = low + n - jnp.where(second, WIN, 0)
    chain = []
    for q in range(2):
        real, imag = band_parts(interp_ref, offsets_ref, 1, bits[0], q, rows)
        left = jnp.where(second, -imag, real)
        right = jnp.where(second, real, imag)
        chain.append(jnp.concatenate([left, right], axis=1))
    chain = jnp.concatenate(chain, axis=0)
    for level in range(2, 4):
        grown = []
        for q in range(2):
            step = band_t(interp_ref, offsets_ref, level, bits[level - 1], q, 0, A)
            grown.append(jnp.dot(chain.astype(BF16), step, preferred_element_type=F32))
        chain = jnp.concatenate(grown, axis=0)
    chain = chain.reshape(N_Y, FAR_ROWS, 2 * A)
    first = chain[:, :MAIN].reshape(N_Y * MAIN, 2 * A)
    rest = chain[:, MAIN:].reshape(N_Y * 8, 2 * A)
    full_ref[...] = jnp.concatenate([first, rest], axis=0).T
    half_rows(full_ref, far_ref, lax.axis_index("h"))


def last_kernel(after_ref, interp_ref, offsets_ref, last_ref):
    del after_ref
    mine = lax.axis_index("h")
    low = mine * (A - HALF)
    last = [
        band_t(interp_ref, offsets_ref, 4, mine, mine, low, HALF),
        band_t(interp_ref, offsets_ref, 4, mine, 1 - mine, low, HALF),
    ]
    last_ref[...] = jnp.concatenate(last, axis=0).T


def merge_kernel(after_ref, near_ref, own_ref, other_ref, out_ref):
    del after_ref
    size = N_Y * PER * REST
    order = one_hot(size, size, lambda r, c: c == r // 4 % 4 * (N_Y * REST) + r // 16 * 4 + r % 4)
    data = jnp.concatenate([own_ref[...], other_ref[...]], axis=0)
    made = jnp.dot(near_ref[...], data, preferred_element_type=F32)
    made = made.astype(BF16)
    for y in range(N_Y):
        for j in range(PER):
            out_ref[y, MAIN * j : MAIN * j + MAIN] = made[MAIN * y : MAIN * y + MAIN, 128 * j : 128 * j + 128]
    rest = made[N_Y * MAIN :]
    rest = jnp.concatenate([rest[:, 128 * j : 128 * j + 128] for j in range(PER)], axis=0)
    rest = jnp.dot(order, rest, preferred_element_type=F32).astype(BF16)
    for y in range(N_Y):
        out_ref[y, PER * MAIN :] = rest[16 * y : 16 * y + 16]


def join_kernel(far_ref, got_ref, send_ref, own_ref):
    order = one_hot(
        PER * N_Y * 8,
        N_Y * 16,
        lambda r, c: (c == r // 8 % N_Y * 16 + r // (8 * N_Y) * 4 + r % 8) & (r % 8 < REST),
    )
    rest = got_ref[:, PER * MAIN :, :].reshape(N_Y * 16, KTAP)
    rest = jnp.dot(order, rest, preferred_element_type=F32).astype(BF16)
    for j in range(PER):
        block = got_ref[:, MAIN * j : MAIN * j + MAIN, :].reshape(N_Y * MAIN, KTAP)
        block = jnp.concatenate([block, rest[8 * N_Y * j : 8 * N_Y * (j + 1)]], axis=0)
        made = jnp.dot(far_ref[...], block, preferred_element_type=F32).astype(BF16)
        send_ref[:, 128 * j : 128 * j + 128] = made[: 2 * HALF]
        own_ref[:, 128 * j : 128 * j + 128] = made[2 * HALF :]


def final_kernel(last_ref, own_ref, other_ref, out_ref):
    data = jnp.concatenate([own_ref[...], other_ref[...]], axis=0)
    made = jnp.dot(last_ref[...], data, preferred_element_type=F32).astype(BF16)
    out_ref[0] = made[:A]
    out_ref[1] = made[A:]


def call(body, ins, outs, scratch=(), limit=48):
    return pl.pallas_call(
        body,
        out_shape=[jax.ShapeDtypeStruct(shape, BF16) for shape in outs],
        in_specs=ins,
        out_specs=[VMEM] * len(outs),
        scratch_shapes=list(scratch),
        compiler_params=pltpu.CompilerParams(vmem_limit_bytes=limit * 2**20),
    )


def shards(raw, chirp, steer, offsets, interp, owner):
    x = raw.reshape(P_HERE, CH, 2, BLOCKS, KTAP).transpose(0, 1, 3, 2, 4)
    x = x.reshape(P_HERE, CH, 2 * BLOCKS, KTAP)
    packed, token = call(
        compress_kernel,
        [HBM] * 3,
        [(N_TILE, PER, 2, P_HERE, KTAP), (16, KTAP)],
        [
            pltpu.SMEM((N_TILE,), jnp.int32),
            pltpu.VMEM((CH, 2, KTAP), BF16),
            pltpu.VMEM((P_HERE, CH, 2 * BLOCKS, KTAP), BF16),
            pltpu.SMEM((N_TILE,), jnp.int32),
            pltpu.VMEM((4 * CH * KTAP, 2 * KTAP), BF16),
            pltpu.VMEM(((BLOCKS + 1) * P_HERE, 2 * CH * KTAP), BF16),
            pltpu.SemaphoreType.DMA((BLOCKS // 8 + 2,)),
        ],
        limit=60,
    )(owner, chirp, x)
    packed = packed.reshape(N_TILE, PER * 2 * P_HERE, KTAP)
    got = lax.all_to_all(packed, ("x", "l"), 0, 0, tiled=True)
    weights, near = call(
        prep_kernel,
        [VMEM] * 5,
        [(4 * HALF, 2 * P_G), (N_Y * (MAIN + REST), 4 * HALF)],
        [pltpu.VMEM((2 * A, 2 * P_G), F32)],
    )(token, steer, interp, offsets, jnp.asarray(row_pick()))
    send, own = call(project_kernel, [VMEM] * 2, [(2 * HALF, R)] * 2)(weights, got)
    other = lax.ppermute(send, "c", [(0, 1), (1, 0)])
    (far,) = call(
        far_kernel,
        [VMEM] * 3,
        [(4 * HALF, N_Y * FAR_ROWS)],
        [pltpu.VMEM((2 * A, N_Y * FAR_ROWS), F32)],
    )(own, interp, offsets)
    (pieces,) = call(merge_kernel, [VMEM] * 4, [(N_Y, PIECE, KTAP)])(far, near, own, other)
    parts = lax.all_to_all(pieces, "y", 0, 0, tiled=True)
    send, own = call(join_kernel, [VMEM] * 2, [(2 * HALF, R)] * 2)(far, parts)
    other = lax.ppermute(send, "h", [(0, 1), (1, 0)])
    (last,) = call(last_kernel, [VMEM] * 3, [(2 * A, 4 * HALF)])(own, interp, offsets)
    (image,) = call(final_kernel, [VMEM] * 3, [(2, A, R)])(last, own, other)
    return image


def solution(mesh):
    split = Mesh(mesh.devices.reshape(2, 8, 2, 4, 4), ("h", "y", "c", "x", "l"))
    pulse = ("h", "y", "c")
    tile = ("x", "l")
    placed = (P(pulse + tile, None, None, None), P(), P(pulse, None), P(), P(), P())
    return jax.shard_map(
        shards, mesh=split, in_specs=placed, out_specs=P(None, pulse, tile), check_vma=False
    )
```

time: 77.3 us -> 71.9 us (0.930)
  blocking collectives: 36.9 us -> 21.6 us
  starting transfers between devices: 11.7 us -> 20 us
  waiting for transfers between devices: 16.4 us -> 20.4 us
  local copies, waits for them, and re-layouts: 3.85 us -> 0.7 us
  Pallas kernels: 7.83 us -> 8.77 us
    all_to_all x1, blocking collectives: 36.9 us -> 21.6 us  [shards(): parts = lax.all_to_all(pieces, 'y', 0, 0, tiled=True)]
    ppermute x0 -> x1, starting transfers between devices: none -> 8.22 us  [shards(): other = lax.ppermute(send, 'h', [(0, 1), (1, 0)])]
    ppermute x0 -> x1, waiting for transfers between devices: none -> 4.58 us  [shards(): other = lax.ppermute(send, 'h', [(0, 1), (1, 0)])]
    unnamed x18 -> x10, local copies, waits for them, and re-layouts: 3.85 us -> 0.7 us
    all_to_all x1, waiting for transfers between devices: 16.4 us -> 15.1 us  [shards(): got = lax.all_to_all(packed, ('x', 'l'), 0, 0, tiled=True)]
    pallas_call x5 -> x8, Pallas kernels: 7.83 us -> 8.77 us  [the longest x1 4.93 us: shards(): call(compress_kernel, [HBM] * 3, [(N_TILE, PER, 2, P_HERE, KTAP), (16, KT...]
  transfers between devices with their start and end apart: 2 -> 3, of which waited for: 1 -> 3; matrix products, arithmetic and copies ran while one was open for 0% -> 0% of each run, Pallas kernels for 2% -> 2%
where the time goes in v2:
time: 71.9 us; the launch traced here: 71.6 us
  blocking collectives  21.6 us (30%)
  waiting for transfers between devices  20.4 us (28%)
  starting transfers between devices  20 us (28%)
  Pallas kernels  8.77 us (12%)
    all_to_all x1, blocking collectives, shards(): parts = lax.all_to_all(pieces, 'y', 0, 0, tiled=True)  21.6 us
    all_to_all x1, waiting for transfers between devices, shards(): got = lax.all_to_all(packed, ('x', 'l'), 0, 0, tiled=True)  15.1 us
    all_to_all x1, starting transfers between devices, shards(): got = lax.all_to_all(packed, ('x', 'l'), 0, 0, tiled=True)  9.83 us
    ppermute x1, starting transfers between devices, shards(): other = lax.ppermute(send, 'h', [(0, 1), (1, 0)])  8.22 us
    pallas_call x1, Pallas kernels, shards(): call(compress_kernel, [HBM] * 3, [(N_TILE, PER, 2, P_HERE, KTAP), (16, KT...  4.93 us
    ppermute x1, waiting for transfers between devices, shards(): other = lax.ppermute(send, 'h', [(0, 1), (1, 0)])  4.58 us
    ppermute x1, starting transfers between devices, shards(): other = lax.ppermute(send, 'c', [(0, 1), (1, 0)])  1.92 us
  transfers between devices with their start and end apart: 3, of which 3 were waited for; matrix products, arithmetic and copies ran while one was open for 0% of the time, Pallas kernels for 2%

profile of v2, /device:TPU:8, one launch (start us, length us, event | category | flops | bytes accessed | tf_op | source)
XLA Modules:
  0.0 71.6 jit_solution(1314070696810689643)
XLA Ops:
  0.0 0.0 copy-start.1
  0.0 0.0 copy-start
  0.0 0.0 copy-start.3
  0.0 0.0 copy-start.2
  0.0 4.9 %shard_map.73 = (bf16[16,4,2,16,128]{4,3,2,1,0:T(8,128)(2,1)}, bf16[16,128]{1,0:T(8,128)(2,1)}) custom-call(s32[16]{0:T(128)} %owner_hbm.1, bf16[4,2,128]{2,1,0:T(2,128)(2,1)} %chirp_hbm.1, bf16[16,4,128,128]{3,2,1,0:T(8,128)(2,1)} %bitcast.6), custom_call_target="tpu_custom_call" | custom-call | tf_op jit(solution)/shard_map/pallas_call | solution.py:294
  5.0 9.8 %all-to-all-start = ((bf16[16,128,128]{2,1,0:T(8,128)(2,1)}), bf16[16,128,128]{2,1,0:T(8,128)(2,1)S(1)}, u32[]{:S(2)}, u32[]{:S(2)}) async-start(bf16[16,128,128]{2,1,0:T(8,128)(2,1)} %bitcast.7), calls=%async_computation | async-start | bytes 1048576 | tf_op jit(solution)/shard_map/all_to_all | solution.py:310
  14.8 0.0 copy-done.1
  14.8 0.0 copy-done
  14.8 0.0 copy-done.3
  14.8 0.0 copy-done.2
  14.8 0.0 copy-start.4
  14.8 0.7 copy-done.4
  15.5 0.7 shard_map.74
  16.2 15.1 %all-to-all-done.got_ref = bf16[16,128,128]{2,1,0:T(8,128)(2,1)S(1)} async-done(((bf16[16,128,128]{2,1,0:T(8,128)(2,1)}), bf16[16,128,128]{2,1,0:T(8,128)(2,1)S(1)}, u32[]{:S(2)}, u32[]{:S(2)}) %all-to-all-start) | async-done | bytes 524320 | tf_op jit(solution)/shard_map/all_to_all | solution.py:310
  31.3 0.5 shard_map.75
  31.8 1.9 %collective-permute-start = (bf16[144,512]{1,0:T(8,128)(2,1)S(1)}, bf16[144,512]{1,0:T(8,128)(2,1)S(1)}, u32[]{:S(2)}, u32[]{:S(2)}) collective-permute-start(bf16[144,512]{1,0:T(8,128)(2,1)S(1)} %get-tuple-element.18), channel_id=1, source_target_pairs={{0,16},{16,0},{1,17},{17,1},{2,18},{18,2},{3,19},{19,3},{4,20},{20... | collective-permute-start | bytes 442376 | tf_op jit(solution)/shard_map/ppermute | solution.py:318
  33.7 0.6 shard_map.76.after_ref.far_ref
  34.3 0.7 %collective-permute-done.other_ref = bf16[144,512]{1,0:T(8,128)(2,1)S(1)} collective-permute-done((bf16[144,512]{1,0:T(8,128)(2,1)S(1)}, bf16[144,512]{1,0:T(8,128)(2,1)S(1)}, u32[]{:S(2)}, u32[]{:S(2)}) %collective-permute-start) | collective-permute-done | bytes 147488 | tf_op jit(solution)/shard_map/ppermute | solution.py:318
  35.0 0.5 shard_map.77
  35.5 21.6 %all_to_all.10.got_ref = bf16[8,208,128]{2,1,0:T(8,128)(2,1)S(1)} all-to-all(bf16[8,208,128]{2,1,0:T(8,128)(2,1)S(1)} %shard_map.77), channel_id=1, replica_groups=mesh['h'=2,'y'=8,'c'=2,'x'=4,'l'=4] {'y'}, dimensions={0} | all-to-all | bytes 851968 | tf_op jit(solution)/shard_map/all_to_all | solution.py:326
  57.1 0.5 shard_map.78
  57.6 8.2 %collective-permute-start.1 = (bf16[144,512]{1,0:T(8,128)(2,1)S(1)}, bf16[144,512]{1,0:T(8,128)(2,1)S(1)}, u32[]{:S(2)}, u32[]{:S(2)}) collective-permute-start(bf16[144,512]{1,0:T(8,128)(2,1)S(1)} %get-tuple-element.20), channel_id=1, source_target_pairs={{0,256},{256,0},{1,257},{257,1},{2,258},{258,2},{3,259},{259,3},{4... | collective-permute-start | bytes 442376 | tf_op jit(solution)/shard_map/ppermute | solution.py:328
  65.9 0.1 shard_map.79.last_ref
  66.0 4.6 %collective-permute-done.1.other_ref = bf16[144,512]{1,0:T(8,128)(2,1)S(1)} collective-permute-done((bf16[144,512]{1,0:T(8,128)(2,1)S(1)}, bf16[144,512]{1,0:T(8,128)(2,1)S(1)}, u32[]{:S(2)}, u32[]{:S(2)}) %collective-permute-start.1) | collective-permute-done | bytes 147488 | tf_op jit(solution)/shard_map/ppermute | solution.py:328
  70.6 1.0 %shard_map.80 = bf16[2,128,512]{2,1,0:T(8,128)(2,1)} custom-call(bf16[256,288]{1,0:T(8,128)(2,1)S(1)} %shard_map.79.last_ref, bf16[144,512]{1,0:T(8,128)(2,1)S(1)} %get-tuple-element.19.after_ref.own_ref, bf16[144,512]{1,0:T(8,128)(2,1)S(1)} %collective-permute-done.1.other_ref), custom_call_target="tpu_custom_call" | custom-call | tf_op jit(solution)/shard_map/pallas_call | solution.py:330
Async XLA Ops:
  0.0 14.8 %copy-start.1 = (bf16[416,256]{1,0:T(8,128)(2,1)S(1)}, bf16[416,256]{1,0:T(8,128)(2,1)}, u32[]{:S(2)}) copy-start(bf16[416,256]{1,0:T(8,128)(2,1)} %constant.2.clone.pick_ref) | copy-start | bytes 638980
  0.0 14.8 %copy-start = (bf16[5,2,2,4,2,128]{5,4,3,2,1,0:T(2,128)(2,1)S(1)}, bf16[5,2,2,4,2,128]{5,4,3,2,1,0:T(2,128)(2,1)}, u32[]{:S(2)}) copy-start(bf16[5,2,2,4,2,128]{5,4,3,2,1,0:T(2,128)(2,1)} %interp_ref.5) | copy-start | bytes 122884
  0.0 14.8 %copy-start.3 = (s32[5,2,128]{2,1,0:T(2,128)S(1)}, s32[5,2,128]{2,1,0:T(2,128)}, u32[]{:S(2)}) copy-start(s32[5,2,128]{2,1,0:T(2,128)} %offsets_ref.5) | copy-start | bytes 15364
  0.0 14.8 %copy-start.2 = (f32[256,128]{1,0:T(8,128)S(1)}, f32[256,128]{1,0:T(8,128)}, u32[]{:S(2)}) copy-start(f32[256,128]{1,0:T(8,128)} %steer_ref.1) | copy-start | bytes 393220
  5.0 26.3 %all-to-all-start = ((bf16[16,128,128]{2,1,0:T(8,128)(2,1)}), bf16[16,128,128]{2,1,0:T(8,128)(2,1)S(1)}, u32[]{:S(2)}, u32[]{:S(2)}) async-start(bf16[16,128,128]{2,1,0:T(8,128)(2,1)} %bitcast.7), calls=%async_computation | async-start | bytes 1048576 | tf_op jit(solution)/shard_map/all_to_all | solution.py:310
  14.8 0.7 copy-start.4
  31.8 3.3 %collective-permute-start = (bf16[144,512]{1,0:T(8,128)(2,1)S(1)}, bf16[144,512]{1,0:T(8,128)(2,1)S(1)}, u32[]{:S(2)}, u32[]{:S(2)}) collective-permute-start(bf16[144,512]{1,0:T(8,128)(2,1)S(1)} %get-tuple-element.18), channel_id=1, source_target_pairs={{0,16},{16,0},{1,17},{17,1},{2,18},{18,2},{3,19},{19,3},{4,20},{20... | collective-permute-start | bytes 442376 | tf_op jit(solution)/shard_map/ppermute | solution.py:318
  57.6 12.9 %collective-permute-start.1 = (bf16[144,512]{1,0:T(8,128)(2,1)S(1)}, bf16[144,512]{1,0:T(8,128)(2,1)S(1)}, u32[]{:S(2)}, u32[]{:S(2)}) collective-permute-start(bf16[144,512]{1,0:T(8,128)(2,1)S(1)} %get-tuple-element.20), channel_id=1, source_target_pairs={{0,256},{256,0},{1,257},{257,1},{2,258},{258,2},{3,259},{259,3},{4... | collective-permute-start | bytes 442376 | tf_op jit(solution)/shard_map/ppermute | solution.py:328

commit v3 on v2

--- a/solution.py
+++ b/solution.py
@@ -112,17 +112,7 @@
     owner_load.wait()
     for t in range(N_TILE):
         inv_ref[owner_ref[t]] = t
-    for g in range(steps):
-        loads[g].wait()
-        parts = []
-        for c in range(CH):
-            got = x_ref[:, c, 16 * g : 16 * g + 16, :]
-            parts.append(got.reshape(256, KTAP))
-        moved = jnp.dot(pick, jnp.concatenate(parts, axis=1), preferred_element_type=F32)
-        moved = moved.astype(BF16)
-        z_ref[128 * g : 128 * g + 128, 0:half] = moved[0:128]
-        z_ref[128 * g : 128 * g + 128, half:] = moved[128:256]
-    for m in range(4):
+    def convolve(m):
         lower = z_ref[256 * m : 256 * m + 256, :]
         upper = z_ref[256 * m + 16 : 256 * m + 272, :]
         acc = jnp.dot(lower, table_ref[0 : 2 * half, :], preferred_element_type=F32)
@@ -134,6 +124,30 @@
                 base = 16 * (PER * n + j)
                 for o in range(2):
                     out_ref[to, j, o] = acc[base : base + 16, 128 * o : 128 * o + 128]
+
+
+    def gather(g):
+        parts = []
+        for c in range(CH):
+            got = x_ref[:, c, 16 * g : 16 * g + 16, :]
+            parts.append(got.reshape(256, KTAP))
+        moved = jnp.dot(pick, jnp.concatenate(parts, axis=1), preferred_element_type=F32)
+        moved = moved.astype(BF16)
+        z_ref[128 * g : 128 * g + 128, 0:half] = moved[0:128]
+        z_ref[128 * g : 128 * g + 128, half:] = moved[128:256]
+
+    for load in loads[0:4]:
+        load.wait()
+    for g in range(0, 4):
+        gather(g)
+    for load in loads[4:8]:
+        load.wait()
+    for g in range(4, 8):
+        gather(g)
+    convolve(0)
+    convolve(1)
+    convolve(2)
+    convolve(3)
 
 
 def band_parts(interp_ref, offsets_ref, level, half, child, rows):
@@ -288,10 +302,8 @@
     )
 
 
-def shards(raw, chirp, steer, offsets, interp, owner):
-    x = raw.reshape(P_HERE, CH, 2, BLOCKS, KTAP).transpose(0, 1, 3, 2, 4)
-    x = x.reshape(P_HERE, CH, 2 * BLOCKS, KTAP)
-    packed, token = call(
+def run_compress(owner, chirp, x):
+    return call(
         compress_kernel,
         [HBM] * 3,
         [(N_TILE, PER, 2, P_HERE, KTAP), (16, KTAP)],
@@ -306,6 +318,12 @@
         ],
         limit=60,
     )(owner, chirp, x)
+
+
+def shards(raw, chirp, steer, offsets, interp, owner):
+    x = raw.reshape(P_HERE, CH, 2, BLOCKS, KTAP).transpose(0, 1, 3, 2, 4)
+    x = x.reshape(P_HERE, CH, 2 * BLOCKS, KTAP)
+    packed, token = run_compress(owner, chirp, x)
     packed = packed.reshape(N_TILE, PER * 2 * P_HERE, KTAP)
     got = lax.all_to_all(packed, ("x", "l"), 0, 0, tiled=True)
     weights, near = call(

time: 71.9 us -> 71.1 us (0.989)
  Pallas kernels: 8.77 us -> 7.97 us
    pallas_call x1, Pallas kernels: 4.93 us -> 4.13 us  [run_compress(): call(compress_kernel, [HBM] * 3, [(N_TILE, PER, 2, P_HERE, KTAP), (16, KT...]
where the time goes in v3:
time: 71.1 us; the launch traced here: 70.8 us
  blocking collectives  21.6 us (30%)
  waiting for transfers between devices  20.4 us (29%)
  starting transfers between devices  20 us (28%)
  Pallas kernels  7.97 us (11%)
    all_to_all x1, blocking collectives, shards(): parts = lax.all_to_all(pieces, 'y', 0, 0, tiled=True)  21.6 us
    all_to_all x1, waiting for transfers between devices, shards(): got = lax.all_to_all(packed, ('x', 'l'), 0, 0, tiled=True)  15.1 us
    all_to_all x1, starting transfers between devices, shards(): got = lax.all_to_all(packed, ('x', 'l'), 0, 0, tiled=True)  9.84 us
    ppermute x1, starting transfers between devices, shards(): other = lax.ppermute(send, 'h', [(0, 1), (1, 0)])  8.23 us
    ppermute x1, waiting for transfers between devices, shards(): other = lax.ppermute(send, 'h', [(0, 1), (1, 0)])  4.59 us
    pallas_call x1, Pallas kernels, run_compress(): call(compress_kernel, [HBM] * 3, [(N_TILE, PER, 2, P_HERE, KTAP), (16, KT...  4.13 us
    ppermute x1, starting transfers between devices, shards(): other = lax.ppermute(send, 'c', [(0, 1), (1, 0)])  1.92 us
  transfers between devices with their start and end apart: 3, of which 3 were waited for; matrix products, arithmetic and copies ran while one was open for 0% of the time, Pallas kernels for 2%

profile of v3, /device:TPU:8, one launch (start us, length us, event | category | flops | bytes accessed | tf_op | source)
XLA Modules:
  0.0 70.8 jit_solution(3311989353303522598)
XLA Ops:
  0.0 0.0 copy-start.1
  0.0 0.0 copy-start
  0.0 0.0 copy-start.3
  0.0 0.0 copy-start.2
  0.0 4.1 %shard_map.73 = (bf16[16,4,2,16,128]{4,3,2,1,0:T(8,128)(2,1)}, bf16[16,128]{1,0:T(8,128)(2,1)}) custom-call(s32[16]{0:T(128)} %owner_hbm.1, bf16[4,2,128]{2,1,0:T(2,128)(2,1)} %chirp_hbm.1, bf16[16,4,128,128]{3,2,1,0:T(8,128)(2,1)} %bitcast.6), custom_call_target="tpu_custom_call" | custom-call | tf_op jit(solution)/shard_map/pallas_call | solution.py:306
  4.2 9.8 %all-to-all-start = ((bf16[16,128,128]{2,1,0:T(8,128)(2,1)}), bf16[16,128,128]{2,1,0:T(8,128)(2,1)S(1)}, u32[]{:S(2)}, u32[]{:S(2)}) async-start(bf16[16,128,128]{2,1,0:T(8,128)(2,1)} %bitcast.7), calls=%async_computation | async-start | bytes 1048576 | tf_op jit(solution)/shard_map/all_to_all | solution.py:328
  14.0 0.0 copy-done.1
  14.0 0.0 copy-done
  14.0 0.0 copy-done.3
  14.0 0.0 copy-done.2
  14.0 0.0 copy-start.4
  14.1 0.7 copy-done.4
  14.7 0.7 shard_map.74
  15.4 15.1 %all-to-all-done.got_ref = bf16[16,128,128]{2,1,0:T(8,128)(2,1)S(1)} async-done(((bf16[16,128,128]{2,1,0:T(8,128)(2,1)}), bf16[16,128,128]{2,1,0:T(8,128)(2,1)S(1)}, u32[]{:S(2)}, u32[]{:S(2)}) %all-to-all-start) | async-done | bytes 524320 | tf_op jit(solution)/shard_map/all_to_all | solution.py:328
  30.5 0.5 shard_map.75
  31.0 1.9 %collective-permute-start = (bf16[144,512]{1,0:T(8,128)(2,1)S(1)}, bf16[144,512]{1,0:T(8,128)(2,1)S(1)}, u32[]{:S(2)}, u32[]{:S(2)}) collective-permute-start(bf16[144,512]{1,0:T(8,128)(2,1)S(1)} %get-tuple-element.18), channel_id=1, source_target_pairs={{0,16},{16,0},{1,17},{17,1},{2,18},{18,2},{3,19},{19,3},{4,20},{20... | collective-permute-start | bytes 442376 | tf_op jit(solution)/shard_map/ppermute | solution.py:336
  32.9 0.6 shard_map.76.after_ref.far_ref
  33.5 0.7 %collective-permute-done.other_ref = bf16[144,512]{1,0:T(8,128)(2,1)S(1)} collective-permute-done((bf16[144,512]{1,0:T(8,128)(2,1)S(1)}, bf16[144,512]{1,0:T(8,128)(2,1)S(1)}, u32[]{:S(2)}, u32[]{:S(2)}) %collective-permute-start) | collective-permute-done | bytes 147488 | tf_op jit(solution)/shard_map/ppermute | solution.py:336
  34.2 0.5 shard_map.77
  34.7 21.6 %all_to_all.10.got_ref = bf16[8,208,128]{2,1,0:T(8,128)(2,1)S(1)} all-to-all(bf16[8,208,128]{2,1,0:T(8,128)(2,1)S(1)} %shard_map.77), channel_id=1, replica_groups=mesh['h'=2,'y'=8,'c'=2,'x'=4,'l'=4] {'y'}, dimensions={0} | all-to-all | bytes 851968 | tf_op jit(solution)/shard_map/all_to_all | solution.py:344
  56.3 0.5 shard_map.78
  56.8 8.2 %collective-permute-start.1 = (bf16[144,512]{1,0:T(8,128)(2,1)S(1)}, bf16[144,512]{1,0:T(8,128)(2,1)S(1)}, u32[]{:S(2)}, u32[]{:S(2)}) collective-permute-start(bf16[144,512]{1,0:T(8,128)(2,1)S(1)} %get-tuple-element.20), channel_id=1, source_target_pairs={{0,256},{256,0},{1,257},{257,1},{2,258},{258,2},{3,259},{259,3},{4... | collective-permute-start | bytes 442376 | tf_op jit(solution)/shard_map/ppermute | solution.py:346
  65.1 0.1 shard_map.79.last_ref
  65.2 4.6 %collective-permute-done.1.other_ref = bf16[144,512]{1,0:T(8,128)(2,1)S(1)} collective-permute-done((bf16[144,512]{1,0:T(8,128)(2,1)S(1)}, bf16[144,512]{1,0:T(8,128)(2,1)S(1)}, u32[]{:S(2)}, u32[]{:S(2)}) %collective-permute-start.1) | collective-permute-done | bytes 147488 | tf_op jit(solution)/shard_map/ppermute | solution.py:346
  69.8 1.0 %shard_map.80 = bf16[2,128,512]{2,1,0:T(8,128)(2,1)} custom-call(bf16[256,288]{1,0:T(8,128)(2,1)S(1)} %shard_map.79.last_ref, bf16[144,512]{1,0:T(8,128)(2,1)S(1)} %get-tuple-element.19.after_ref.own_ref, bf16[144,512]{1,0:T(8,128)(2,1)S(1)} %collective-permute-done.1.other_ref), custom_call_target="tpu_custom_call" | custom-call | tf_op jit(solution)/shard_map/pallas_call | solution.py:348
Async XLA Ops:
  0.0 14.0 %copy-start.1 = (bf16[416,256]{1,0:T(8,128)(2,1)S(1)}, bf16[416,256]{1,0:T(8,128)(2,1)}, u32[]{:S(2)}) copy-start(bf16[416,256]{1,0:T(8,128)(2,1)} %constant.2.clone.pick_ref) | copy-start | bytes 638980
  0.0 14.0 %copy-start = (bf16[5,2,2,4,2,128]{5,4,3,2,1,0:T(2,128)(2,1)S(1)}, bf16[5,2,2,4,2,128]{5,4,3,2,1,0:T(2,128)(2,1)}, u32[]{:S(2)}) copy-start(bf16[5,2,2,4,2,128]{5,4,3,2,1,0:T(2,128)(2,1)} %interp_ref.5) | copy-start | bytes 122884
  0.0 14.0 %copy-start.3 = (s32[5,2,128]{2,1,0:T(2,128)S(1)}, s32[5,2,128]{2,1,0:T(2,128)}, u32[]{:S(2)}) copy-start(s32[5,2,128]{2,1,0:T(2,128)} %offsets_ref.5) | copy-start | bytes 15364
  0.0 14.0 %copy-start.2 = (f32[256,128]{1,0:T(8,128)S(1)}, f32[256,128]{1,0:T(8,128)}, u32[]{:S(2)}) copy-start(f32[256,128]{1,0:T(8,128)} %steer_ref.1) | copy-start | bytes 393220
  4.2 26.4 %all-to-all-start = ((bf16[16,128,128]{2,1,0:T(8,128)(2,1)}), bf16[16,128,128]{2,1,0:T(8,128)(2,1)S(1)}, u32[]{:S(2)}, u32[]{:S(2)}) async-start(bf16[16,128,128]{2,1,0:T(8,128)(2,1)} %bitcast.7), calls=%async_computation | async-start | bytes 1048576 | tf_op jit(solution)/shard_map/all_to_all | solution.py:328
  14.0 0.7 copy-start.4
  31.0 3.3 %collective-permute-start = (bf16[144,512]{1,0:T(8,128)(2,1)S(1)}, bf16[144,512]{1,0:T(8,128)(2,1)S(1)}, u32[]{:S(2)}, u32[]{:S(2)}) collective-permute-start(bf16[144,512]{1,0:T(8,128)(2,1)S(1)} %get-tuple-element.18), channel_id=1, source_target_pairs={{0,16},{16,0},{1,17},{17,1},{2,18},{18,2},{3,19},{19,3},{4,20},{20... | collective-permute-start | bytes 442376 | tf_op jit(solution)/shard_map/ppermute | solution.py:336
  56.8 13.0 %collective-permute-start.1 = (bf16[144,512]{1,0:T(8,128)(2,1)S(1)}, bf16[144,512]{1,0:T(8,128)(2,1)S(1)}, u32[]{:S(2)}, u32[]{:S(2)}) collective-permute-start(bf16[144,512]{1,0:T(8,128)(2,1)S(1)} %get-tuple-element.20), channel_id=1, source_target_pairs={{0,256},{256,0},{1,257},{257,1},{2,258},{258,2},{3,259},{259,3},{4... | collective-permute-start | bytes 442376 | tf_op jit(solution)/shard_map/ppermute | solution.py:346

commit v4 on v3

--- a/solution.py
+++ b/solution.py
@@ -195,11 +195,12 @@
 
 
 def half_rows(full_ref, out_ref, mine):
-    for n, side in enumerate((1 - mine, mine)):
+    rows = []
+    for side in (1 - mine, mine):
         for part in range(2):
             low = pl.multiple_of(part * A + side * (A - HALF), 8)
-            at = (2 * n + part) * HALF
-            out_ref[at : at + HALF, :] = full_ref[pl.ds(low, HALF), :].astype(BF16)
+            rows.append(full_ref[pl.ds(low, HALF), :])
+    out_ref[...] = jnp.concatenate(rows, axis=0).astype(BF16)
 
 
 def project_kernel(weights_ref, got_ref, send_ref, own_ref):

time: 71.1 us -> 71.1 us (level)
  no operation moved by 1% of the time
where the time goes in v4:
time: 71.1 us; the launch traced here: 70.8 us
  blocking collectives  21.6 us (30%)
  waiting for transfers between devices  20.4 us (29%)
  starting transfers between devices  20 us (28%)
  Pallas kernels  7.97 us (11%)
    all_to_all x1, blocking collectives, shards(): parts = lax.all_to_all(pieces, 'y', 0, 0, tiled=True)  21.6 us
    all_to_all x1, waiting for transfers between devices, shards(): got = lax.all_to_all(packed, ('x', 'l'), 0, 0, tiled=True)  15.1 us
    all_to_all x1, starting transfers between devices, shards(): got = lax.all_to_all(packed, ('x', 'l'), 0, 0, tiled=True)  9.84 us
    ppermute x1, starting transfers between devices, shards(): other = lax.ppermute(send, 'h', [(0, 1), (1, 0)])  8.23 us
    ppermute x1, waiting for transfers between devices, shards(): other = lax.ppermute(send, 'h', [(0, 1), (1, 0)])  4.59 us
    pallas_call x1, Pallas kernels, run_compress(): call(compress_kernel, [HBM] * 3, [(N_TILE, PER, 2, P_HERE, KTAP), (16, KT...  4.13 us
    ppermute x1, starting transfers between devices, shards(): other = lax.ppermute(send, 'c', [(0, 1), (1, 0)])  1.92 us
  transfers between devices with their start and end apart: 3, of which 3 were waited for; matrix products, arithmetic and copies ran while one was open for 0% of the time, Pallas kernels for 2%

profile of v4, /device:TPU:8, one launch (start us, length us, event | category | flops | bytes accessed | tf_op | source)
XLA Modules:
  0.0 70.8 jit_solution(2329006930463155809)
XLA Ops:
  0.0 0.0 copy-start.1
  0.0 0.0 copy-start
  0.0 0.0 copy-start.3
  0.0 0.0 copy-start.2
  0.0 4.1 %shard_map.73 = (bf16[16,4,2,16,128]{4,3,2,1,0:T(8,128)(2,1)}, bf16[16,128]{1,0:T(8,128)(2,1)}) custom-call(s32[16]{0:T(128)} %owner_hbm.1, bf16[4,2,128]{2,1,0:T(2,128)(2,1)} %chirp_hbm.1, bf16[16,4,128,128]{3,2,1,0:T(8,128)(2,1)} %bitcast.6), custom_call_target="tpu_custom_call" | custom-call | tf_op jit(solution)/shard_map/pallas_call | solution.py:307
  4.2 9.8 %all-to-all-start = ((bf16[16,128,128]{2,1,0:T(8,128)(2,1)}), bf16[16,128,128]{2,1,0:T(8,128)(2,1)S(1)}, u32[]{:S(2)}, u32[]{:S(2)}) async-start(bf16[16,128,128]{2,1,0:T(8,128)(2,1)} %bitcast.7), calls=%async_computation | async-start | bytes 1048576 | tf_op jit(solution)/shard_map/all_to_all | solution.py:329
  14.0 0.0 copy-done.1
  14.0 0.0 copy-done
  14.0 0.0 copy-done.3
  14.0 0.0 copy-done.2
  14.0 0.0 copy-start.4
  14.1 0.7 copy-done.4
  14.7 0.7 shard_map.74
  15.4 15.1 %all-to-all-done.got_ref = bf16[16,128,128]{2,1,0:T(8,128)(2,1)S(1)} async-done(((bf16[16,128,128]{2,1,0:T(8,128)(2,1)}), bf16[16,128,128]{2,1,0:T(8,128)(2,1)S(1)}, u32[]{:S(2)}, u32[]{:S(2)}) %all-to-all-start) | async-done | bytes 524320 | tf_op jit(solution)/shard_map/all_to_all | solution.py:329
  30.5 0.5 shard_map.75
  31.0 1.9 %collective-permute-start = (bf16[144,512]{1,0:T(8,128)(2,1)S(1)}, bf16[144,512]{1,0:T(8,128)(2,1)S(1)}, u32[]{:S(2)}, u32[]{:S(2)}) collective-permute-start(bf16[144,512]{1,0:T(8,128)(2,1)S(1)} %get-tuple-element.18), channel_id=1, source_target_pairs={{0,16},{16,0},{1,17},{17,1},{2,18},{18,2},{3,19},{19,3},{4,20},{20... | collective-permute-start | bytes 442376 | tf_op jit(solution)/shard_map/ppermute | solution.py:337
  32.9 0.6 shard_map.76.after_ref.far_ref
  33.5 0.7 %collective-permute-done.other_ref = bf16[144,512]{1,0:T(8,128)(2,1)S(1)} collective-permute-done((bf16[144,512]{1,0:T(8,128)(2,1)S(1)}, bf16[144,512]{1,0:T(8,128)(2,1)S(1)}, u32[]{:S(2)}, u32[]{:S(2)}) %collective-permute-start) | collective-permute-done | bytes 147488 | tf_op jit(solution)/shard_map/ppermute | solution.py:337
  34.2 0.5 shard_map.77
  34.7 21.6 %all_to_all.10.got_ref = bf16[8,208,128]{2,1,0:T(8,128)(2,1)S(1)} all-to-all(bf16[8,208,128]{2,1,0:T(8,128)(2,1)S(1)} %shard_map.77), channel_id=1, replica_groups=mesh['h'=2,'y'=8,'c'=2,'x'=4,'l'=4] {'y'}, dimensions={0} | all-to-all | bytes 851968 | tf_op jit(solution)/shard_map/all_to_all | solution.py:345
  56.3 0.5 shard_map.78
  56.8 8.2 %collective-permute-start.1 = (bf16[144,512]{1,0:T(8,128)(2,1)S(1)}, bf16[144,512]{1,0:T(8,128)(2,1)S(1)}, u32[]{:S(2)}, u32[]{:S(2)}) collective-permute-start(bf16[144,512]{1,0:T(8,128)(2,1)S(1)} %get-tuple-element.20), channel_id=1, source_target_pairs={{0,256},{256,0},{1,257},{257,1},{2,258},{258,2},{3,259},{259,3},{4... | collective-permute-start | bytes 442376 | tf_op jit(solution)/shard_map/ppermute | solution.py:347
  65.1 0.1 shard_map.79.last_ref
  65.2 4.6 %collective-permute-done.1.other_ref = bf16[144,512]{1,0:T(8,128)(2,1)S(1)} collective-permute-done((bf16[144,512]{1,0:T(8,128)(2,1)S(1)}, bf16[144,512]{1,0:T(8,128)(2,1)S(1)}, u32[]{:S(2)}, u32[]{:S(2)}) %collective-permute-start.1) | collective-permute-done | bytes 147488 | tf_op jit(solution)/shard_map/ppermute | solution.py:347
  69.8 1.0 %shard_map.80 = bf16[2,128,512]{2,1,0:T(8,128)(2,1)} custom-call(bf16[256,288]{1,0:T(8,128)(2,1)S(1)} %shard_map.79.last_ref, bf16[144,512]{1,0:T(8,128)(2,1)S(1)} %get-tuple-element.19.after_ref.own_ref, bf16[144,512]{1,0:T(8,128)(2,1)S(1)} %collective-permute-done.1.other_ref), custom_call_target="tpu_custom_call" | custom-call | tf_op jit(solution)/shard_map/pallas_call | solution.py:349
Async XLA Ops:
  0.0 14.0 %copy-start.1 = (bf16[416,256]{1,0:T(8,128)(2,1)S(1)}, bf16[416,256]{1,0:T(8,128)(2,1)}, u32[]{:S(2)}) copy-start(bf16[416,256]{1,0:T(8,128)(2,1)} %constant.2.clone.pick_ref) | copy-start | bytes 638980
  0.0 14.0 %copy-start = (bf16[5,2,2,4,2,128]{5,4,3,2,1,0:T(2,128)(2,1)S(1)}, bf16[5,2,2,4,2,128]{5,4,3,2,1,0:T(2,128)(2,1)}, u32[]{:S(2)}) copy-start(bf16[5,2,2,4,2,128]{5,4,3,2,1,0:T(2,128)(2,1)} %interp_ref.5) | copy-start | bytes 122884
  0.0 14.0 %copy-start.3 = (s32[5,2,128]{2,1,0:T(2,128)S(1)}, s32[5,2,128]{2,1,0:T(2,128)}, u32[]{:S(2)}) copy-start(s32[5,2,128]{2,1,0:T(2,128)} %offsets_ref.5) | copy-start | bytes 15364
  0.0 14.0 %copy-start.2 = (f32[256,128]{1,0:T(8,128)S(1)}, f32[256,128]{1,0:T(8,128)}, u32[]{:S(2)}) copy-start(f32[256,128]{1,0:T(8,128)} %steer_ref.1) | copy-start | bytes 393220
  4.2 26.4 %all-to-all-start = ((bf16[16,128,128]{2,1,0:T(8,128)(2,1)}), bf16[16,128,128]{2,1,0:T(8,128)(2,1)S(1)}, u32[]{:S(2)}, u32[]{:S(2)}) async-start(bf16[16,128,128]{2,1,0:T(8,128)(2,1)} %bitcast.7), calls=%async_computation | async-start | bytes 1048576 | tf_op jit(solution)/shard_map/all_to_all | solution.py:329
  14.0 0.7 copy-start.4
  31.0 3.3 %collective-permute-start = (bf16[144,512]{1,0:T(8,128)(2,1)S(1)}, bf16[144,512]{1,0:T(8,128)(2,1)S(1)}, u32[]{:S(2)}, u32[]{:S(2)}) collective-permute-start(bf16[144,512]{1,0:T(8,128)(2,1)S(1)} %get-tuple-element.18), channel_id=1, source_target_pairs={{0,16},{16,0},{1,17},{17,1},{2,18},{18,2},{3,19},{19,3},{4,20},{20... | collective-permute-start | bytes 442376 | tf_op jit(solution)/shard_map/ppermute | solution.py:337
  56.8 13.0 %collective-permute-start.1 = (bf16[144,512]{1,0:T(8,128)(2,1)S(1)}, bf16[144,512]{1,0:T(8,128)(2,1)S(1)}, u32[]{:S(2)}, u32[]{:S(2)}) collective-permute-start(bf16[144,512]{1,0:T(8,128)(2,1)S(1)} %get-tuple-element.20), channel_id=1, source_target_pairs={{0,256},{256,0},{1,257},{257,1},{2,258},{258,2},{3,259},{259,3},{4... | collective-permute-start | bytes 442376 | tf_op jit(solution)/shard_map/ppermute | solution.py:347

commit v5 on v4

--- a/solution.py
+++ b/solution.py
@@ -1,3 +1,4 @@
+import functools
 import math
 
 import jax
@@ -203,12 +204,17 @@
     out_ref[...] = jnp.concatenate(rows, axis=0).astype(BF16)
 
 
-def project_kernel(weights_ref, got_ref, send_ref, own_ref):
+def project_kernel(weights_ref, got_ref, out_ref, *, first):
+    weights = weights_ref[first : first + 2 * HALF, :]
     for j in range(PER):
         block = got_ref[:, 32 * j : 32 * j + 32, :].reshape(2 * P_G, KTAP)
-        made = jnp.dot(weights_ref[...], block, preferred_element_type=F32).astype(BF16)
-        send_ref[:, 128 * j : 128 * j + 128] = made[: 2 * HALF]
-        own_ref[:, 128 * j : 128 * j + 128] = made[2 * HALF :]
+        made = jnp.dot(weights, block, preferred_element_type=F32).astype(BF16)
+        out_ref[:, 128 * j : 128 * j + 128] = made
+
+
+def own_kernel(after_ref, weights_ref, got_ref, out_ref):
+    del after_ref
+    project_kernel(weights_ref, got_ref, out_ref, first=2 * HALF)
 
 
 def far_kernel(after_ref, interp_ref, offsets_ref, far_ref, full_ref):
@@ -333,8 +339,10 @@
         [(4 * HALF, 2 * P_G), (N_Y * (MAIN + REST), 4 * HALF)],
         [pltpu.VMEM((2 * A, 2 * P_G), F32)],
     )(token, steer, interp, offsets, jnp.asarray(row_pick()))
-    send, own = call(project_kernel, [VMEM] * 2, [(2 * HALF, R)] * 2)(weights, got)
+    send_rows = functools.partial(project_kernel, first=0)
+    (send,) = call(send_rows, [VMEM] * 2, [(2 * HALF, R)])(weights, got)
     other = lax.ppermute(send, "c", [(0, 1), (1, 0)])
+    (own,) = call(own_kernel, [VMEM] * 3, [(2 * HALF, R)])(send, weights, got)
     (far,) = call(
         far_kernel,
         [VMEM] * 3,

time: 71.1 us -> 70.9 us (level)
  no operation moved by 1% of the time
where the time goes in v5:
time: 70.9 us; the launch traced here: 70.6 us
  blocking collectives  21.6 us (30%)
  waiting for transfers between devices  20.1 us (28%)
  starting transfers between devices  20 us (28%)
  Pallas kernels  8.1 us (11%)
    all_to_all x1, blocking collectives, shards(): parts = lax.all_to_all(pieces, 'y', 0, 0, tiled=True)  21.6 us
    all_to_all x1, waiting for transfers between devices, shards(): got = lax.all_to_all(packed, ('x', 'l'), 0, 0, tiled=True)  15.1 us
    all_to_all x1, starting transfers between devices, shards(): got = lax.all_to_all(packed, ('x', 'l'), 0, 0, tiled=True)  9.84 us
    ppermute x1, starting transfers between devices, shards(): other = lax.ppermute(send, 'h', [(0, 1), (1, 0)])  8.22 us
    ppermute x1, waiting for transfers between devices, shards(): other = lax.ppermute(send, 'h', [(0, 1), (1, 0)])  4.58 us
    pallas_call x1, Pallas kernels, run_compress(): call(compress_kernel, [HBM] * 3, [(N_TILE, PER, 2, P_HERE, KTAP), (16, KT...  4.12 us
    ppermute x1, starting transfers between devices, shards(): other = lax.ppermute(send, 'c', [(0, 1), (1, 0)])  1.92 us
  transfers between devices with their start and end apart: 3, of which 3 were waited for; matrix products, arithmetic and copies ran while one was open for 0% of the time, Pallas kernels for 2%

profile of v5, /device:TPU:8, one launch (start us, length us, event | category | flops | bytes accessed | tf_op | source)
XLA Modules:
  0.0 70.6 jit_solution(16134265310235719974)
XLA Ops:
  0.0 0.0 copy-start.1
  0.0 0.0 copy-start
  0.0 0.0 copy-start.3
  0.0 0.0 copy-start.2
  0.0 4.1 %shard_map.73 = (bf16[16,4,2,16,128]{4,3,2,1,0:T(8,128)(2,1)}, bf16[16,128]{1,0:T(8,128)(2,1)}) custom-call(s32[16]{0:T(128)} %owner_hbm.1, bf16[4,2,128]{2,1,0:T(2,128)(2,1)} %chirp_hbm.1, bf16[16,4,128,128]{3,2,1,0:T(8,128)(2,1)} %bitcast.6), custom_call_target="tpu_custom_call" | custom-call | tf_op jit(solution)/shard_map/pallas_call | solution.py:313
  4.1 9.8 %all-to-all-start = ((bf16[16,128,128]{2,1,0:T(8,128)(2,1)}), bf16[16,128,128]{2,1,0:T(8,128)(2,1)S(1)}, u32[]{:S(2)}, u32[]{:S(2)}) async-start(bf16[16,128,128]{2,1,0:T(8,128)(2,1)} %bitcast.7), calls=%async_computation | async-start | bytes 1048576 | tf_op jit(solution)/shard_map/all_to_all | solution.py:335
  14.0 0.0 copy-done.1
  14.0 0.0 copy-done
  14.0 0.0 copy-done.3
  14.0 0.0 copy-done.2
  14.0 0.0 copy-start.4
  14.0 0.7 copy-done.4
  14.7 0.7 shard_map.74
  15.4 15.1 %all-to-all-done.got_ref = bf16[16,128,128]{2,1,0:T(8,128)(2,1)S(1)} async-done(((bf16[16,128,128]{2,1,0:T(8,128)(2,1)}), bf16[16,128,128]{2,1,0:T(8,128)(2,1)S(1)}, u32[]{:S(2)}, u32[]{:S(2)}) %all-to-all-start) | async-done | bytes 524320 | tf_op jit(solution)/shard_map/all_to_all | solution.py:335
  30.5 0.3 shard_map.75.after_ref
  30.8 1.9 %collective-permute-start = (bf16[144,512]{1,0:T(8,128)(2,1)S(1)}, bf16[144,512]{1,0:T(8,128)(2,1)S(1)}, u32[]{:S(2)}, u32[]{:S(2)}) collective-permute-start(bf16[144,512]{1,0:T(8,128)(2,1)S(1)} %shard_map.75.after_ref), channel_id=1, source_target_pairs={{0,16},{16,0},{1,17},{17,1},{2,18},{18,2},{3,19},{19,3},{4,20},{20... | collective-permute-start | bytes 442376 | tf_op jit(solution)/shard_map/ppermute | solution.py:344
  32.7 0.3 shard_map.76.after_ref.own_ref
  33.0 0.6 shard_map.77.after_ref.far_ref
  33.6 0.4 collective-permute-done.other_ref
  34.1 0.5 shard_map.78
  34.6 21.6 %all_to_all.10.got_ref = bf16[8,208,128]{2,1,0:T(8,128)(2,1)S(1)} all-to-all(bf16[8,208,128]{2,1,0:T(8,128)(2,1)S(1)} %shard_map.78), channel_id=1, replica_groups=mesh['h'=2,'y'=8,'c'=2,'x'=4,'l'=4] {'y'}, dimensions={0} | all-to-all | bytes 851968 | tf_op jit(solution)/shard_map/all_to_all | solution.py:353
  56.2 0.5 shard_map.79
  56.6 8.2 %collective-permute-start.1 = (bf16[144,512]{1,0:T(8,128)(2,1)S(1)}, bf16[144,512]{1,0:T(8,128)(2,1)S(1)}, u32[]{:S(2)}, u32[]{:S(2)}) collective-permute-start(bf16[144,512]{1,0:T(8,128)(2,1)S(1)} %get-tuple-element.16), channel_id=1, source_target_pairs={{0,256},{256,0},{1,257},{257,1},{2,258},{258,2},{3,259},{259,3},{4... | collective-permute-start | bytes 442376 | tf_op jit(solution)/shard_map/ppermute | solution.py:355
  64.9 0.1 shard_map.80.last_ref
  65.0 4.6 %collective-permute-done.1.other_ref = bf16[144,512]{1,0:T(8,128)(2,1)S(1)} collective-permute-done((bf16[144,512]{1,0:T(8,128)(2,1)S(1)}, bf16[144,512]{1,0:T(8,128)(2,1)S(1)}, u32[]{:S(2)}, u32[]{:S(2)}) %collective-permute-start.1) | collective-permute-done | bytes 147488 | tf_op jit(solution)/shard_map/ppermute | solution.py:355
  69.6 1.0 %shard_map.81 = bf16[2,128,512]{2,1,0:T(8,128)(2,1)} custom-call(bf16[256,288]{1,0:T(8,128)(2,1)S(1)} %shard_map.80.last_ref, bf16[144,512]{1,0:T(8,128)(2,1)S(1)} %get-tuple-element.15.after_ref.own_ref, bf16[144,512]{1,0:T(8,128)(2,1)S(1)} %collective-permute-done.1.other_ref), custom_call_target="tpu_custom_call" | custom-call | tf_op jit(solution)/shard_map/pallas_call | solution.py:357
Async XLA Ops:
  0.0 14.0 %copy-start.1 = (bf16[416,256]{1,0:T(8,128)(2,1)S(1)}, bf16[416,256]{1,0:T(8,128)(2,1)}, u32[]{:S(2)}) copy-start(bf16[416,256]{1,0:T(8,128)(2,1)} %constant.2.clone.pick_ref) | copy-start | bytes 638980
  0.0 14.0 %copy-start = (bf16[5,2,2,4,2,128]{5,4,3,2,1,0:T(2,128)(2,1)S(1)}, bf16[5,2,2,4,2,128]{5,4,3,2,1,0:T(2,128)(2,1)}, u32[]{:S(2)}) copy-start(bf16[5,2,2,4,2,128]{5,4,3,2,1,0:T(2,128)(2,1)} %interp_ref.5) | copy-start | bytes 122884
  0.0 14.0 %copy-start.3 = (s32[5,2,128]{2,1,0:T(2,128)S(1)}, s32[5,2,128]{2,1,0:T(2,128)}, u32[]{:S(2)}) copy-start(s32[5,2,128]{2,1,0:T(2,128)} %offsets_ref.5) | copy-start | bytes 15364
  0.0 14.0 %copy-start.2 = (f32[256,128]{1,0:T(8,128)S(1)}, f32[256,128]{1,0:T(8,128)}, u32[]{:S(2)}) copy-start(f32[256,128]{1,0:T(8,128)} %steer_ref.1) | copy-start | bytes 393220
  4.1 26.4 %all-to-all-start = ((bf16[16,128,128]{2,1,0:T(8,128)(2,1)}), bf16[16,128,128]{2,1,0:T(8,128)(2,1)S(1)}, u32[]{:S(2)}, u32[]{:S(2)}) async-start(bf16[16,128,128]{2,1,0:T(8,128)(2,1)} %bitcast.7), calls=%async_computation | async-start | bytes 1048576 | tf_op jit(solution)/shard_map/all_to_all | solution.py:335
  14.0 0.7 copy-start.4
  30.8 3.3 %collective-permute-start = (bf16[144,512]{1,0:T(8,128)(2,1)S(1)}, bf16[144,512]{1,0:T(8,128)(2,1)S(1)}, u32[]{:S(2)}, u32[]{:S(2)}) collective-permute-start(bf16[144,512]{1,0:T(8,128)(2,1)S(1)} %shard_map.75.after_ref), channel_id=1, source_target_pairs={{0,16},{16,0},{1,17},{17,1},{2,18},{18,2},{3,19},{19,3},{4,20},{20... | collective-permute-start | bytes 442376 | tf_op jit(solution)/shard_map/ppermute | solution.py:344
  56.6 12.9 %collective-permute-start.1 = (bf16[144,512]{1,0:T(8,128)(2,1)S(1)}, bf16[144,512]{1,0:T(8,128)(2,1)S(1)}, u32[]{:S(2)}, u32[]{:S(2)}) collective-permute-start(bf16[144,512]{1,0:T(8,128)(2,1)S(1)} %get-tuple-element.16), channel_id=1, source_target_pairs={{0,256},{256,0},{1,257},{257,1},{2,258},{258,2},{3,259},{259,3},{4... | collective-permute-start | bytes 442376 | tf_op jit(solution)/shard_map/ppermute | solution.py:355
